TPU v7x, 256 devices: a whole 4x4x8 slice. The times are simulated.
256 devices in a mesh: row: 8 (over z), col: 32 (over y, x, core).
Axes of the slice: x: 4, y: 4, z: 8, core: 2. Of those that a mesh axis runs over, the one named last changes fastest.
Arguments:
- matrix: bfloat16 [2, 8, 8, 256, 2, 32, 256], P(None, None, 'row', None, None, 'col'), may hold values from -6 to 22
- inverses: bfloat16 [2, 2, 256, 256], replicated, may hold values from -1 to 1
- pivots: int32 [2], replicated, may hold values from 0 to 63, as said below
- col_lists: int32 [2, 64], replicated, may hold values from 0 to 1
- row_lists: int32 [2, 64], replicated, may hold values from 0 to 1
Outputs:
- factored: bfloat16 [2, 8, 8, 256, 2, 32, 256], P(None, None, 'row', None, None, 'col')
Inputs may be any that keep to these rules, and one draw needn't show every extreme that they name: `pivots`: two different tile indices; one of the two steps eliminates the last tile index, 63.
All inputs are finite; a program needn't handle non-finite values.
Results may differ from a plain program's by a relative error of at most 0.0037.
Values may be sent and summed in bfloat16 or wider, within the bound.
A program may use at most 128 MiB of HBM per device.

v0:
```python
import jax
import jax.numpy as jnp
from jax import lax
from jax.sharding import PartitionSpec as P


def spread(value, axis, source):
    kept = jnp.where(lax.axis_index(axis) == source, value, 0).astype(value.dtype)
    return lax.psum(kept, axis)


def complex_product(left_part, right_part):
    real_real = jnp.dot(left_part[0], right_part[0], preferred_element_type=jnp.float32)
    imag_imag = jnp.dot(left_part[1], right_part[1], preferred_element_type=jnp.float32)
    real_imag = jnp.dot(left_part[0], right_part[1], preferred_element_type=jnp.float32)
    imag_real = jnp.dot(left_part[1], right_part[0], preferred_element_type=jnp.float32)
    return jnp.stack([real_real - imag_imag, real_imag + imag_real])


def refine(diagonal, guess_inv):
    product = complex_product(diagonal, guess_inv)
    identity = jnp.eye(diagonal.shape[1], dtype=jnp.float32)
    residue = jnp.stack([2.0 * identity - product[0], -product[1]]).astype(jnp.bfloat16)
    return complex_product(guess_inv, residue).astype(jnp.bfloat16)


def lookup(table, wanted):
    hits = wanted[:, None] == jnp.arange(table.shape[0], dtype=jnp.int32)[None, :]
    return jnp.sum(jnp.where(hits, table[None, :], 0), axis=1) > 0


def eliminate(column, factor, take_rows):

    def mult(left, right):
        return jnp.einsum("rik,kn->rin", left, right, preferred_element_type=jnp.float32)

    real_part = mult(column[0], factor[0]) - mult(column[1], factor[1])
    imag_part = mult(column[0], factor[1]) + mult(column[1], factor[0])
    scaled = jnp.stack([real_part, imag_part]).astype(jnp.bfloat16)
    return jnp.where(take_rows[None, :, None, None], scaled, column)


def trailing(tiles_now, col_panel, upper_rows, update_flags):

    def mult(left, right):
        return jnp.einsum("rik,kcn->ricn", left, right, preferred_element_type=jnp.float32)

    mask = update_flags[:, None, :, None]
    real_part = tiles_now[0].astype(jnp.float32) - (
        mult(col_panel[0], upper_rows[0]) - mult(col_panel[1], upper_rows[1])
    )
    real_new = jnp.where(mask, real_part.astype(jnp.bfloat16), tiles_now[0])
    imag_part = tiles_now[1].astype(jnp.float32) - (
        mult(col_panel[0], upper_rows[1]) + mult(col_panel[1], upper_rows[0])
    )
    imag_new = jnp.where(mask, imag_part.astype(jnp.bfloat16), tiles_now[1])
    return jnp.stack([real_new, imag_new])


def shards(matrix, inverses, pivots, col_lists, row_lists):
    tile_rows = matrix.shape[1]
    tile_width = matrix.shape[3]
    tile_cols = matrix.shape[4]
    tiles_now = matrix.reshape(2, tile_rows, tile_width, tile_cols, tile_width)
    rows_count = lax.axis_size("row")
    cols_count = lax.axis_size("col")
    row_pos = lax.axis_index("row")
    col_pos = lax.axis_index("col")
    row_ids = jnp.arange(tile_rows, dtype=jnp.int32) * rows_count + row_pos
    col_ids = jnp.arange(tile_cols, dtype=jnp.int32) * cols_count + col_pos
    first_pivot = pivots[0]
    for step_no in range(2):
        panels_tiles_now = tiles_now
        pivot_id = pivots[step_no]
        pivot_rowdev = pivot_id % rows_count
        pivot_coldev = pivot_id % cols_count
        local_row = pivot_id // rows_count
        local_col = pivot_id // cols_count
        live_rows = row_ids != pivot_id
        live_cols = col_ids != pivot_id
        if step_no == 1:
            live_rows = live_rows & (row_ids != first_pivot)
            live_cols = live_cols & (col_ids != first_pivot)
        take_rows = lookup(col_lists[step_no], row_ids) & live_rows
        take_cols = lookup(row_lists[step_no], col_ids) & live_cols
        column = lax.dynamic_index_in_dim(panels_tiles_now, local_col, 3, keepdims=False)
        pivot_row = lax.dynamic_index_in_dim(panels_tiles_now, local_row, 1, keepdims=False)
        is_owner = (row_pos == pivot_rowdev) & (col_pos == pivot_coldev)
        diagonal = lax.dynamic_index_in_dim(column, local_row, 1, keepdims=False)
        guess_inv = inverses[step_no]
        factor = lax.cond(
            is_owner, lambda: refine(diagonal, guess_inv), lambda: jnp.zeros_like(guess_inv)
        )
        factor = spread(factor, "row", pivot_rowdev)
        outgoing = lax.cond(
            col_pos == pivot_coldev, lambda: eliminate(column, factor, take_rows), lambda: column
        )
        col_panel = spread(outgoing, "col", pivot_coldev)
        upper_rows = spread(pivot_row, "row", pivot_rowdev)
        at_pivot = (jnp.arange(tile_rows, dtype=jnp.int32) == local_row) & (row_pos == pivot_rowdev)
        written = jnp.where(at_pivot[None, :, None, None], factor[:, None], col_panel)
        new_column = jnp.where(col_pos == pivot_coldev, written, column)
        panels_tiles_now = lax.dynamic_update_index_in_dim(
            panels_tiles_now, new_column, local_col, 3
        )
        update_flags = take_rows[:, None] & take_cols[None, :]
        tiles_now, col_panel, upper_rows, update_flags = (
            panels_tiles_now,
            col_panel,
            upper_rows,
            update_flags,
        )
        tiles_now = trailing(tiles_now, col_panel, upper_rows, update_flags)
    return tiles_now.reshape(matrix.shape)


def solution(mesh):
    in_specs = (P(None, None, "row", None, None, "col", None), P(), P(), P(), P())
    out_specs = P(None, None, "row", None, None, "col", None)
    return jax.shard_map(shards, mesh=mesh, in_specs=in_specs, out_specs=out_specs, check_vma=False)
```

profile of v0, /device:TPU:1, one launch (start us, length us, event | category | flops | bytes accessed | tf_op | source)
XLA Modules:
  0.0 454.7 jit_solution(1692442723888534775)
XLA Ops:
  6.5 1.4 fusion.120
  10.7 1.4 constant_dynamic-slice_fusion
  12.2 0.9 fusion.119
  13.1 0.7 broadcast_select_fusion.3
  13.9 9.1 %constant_dynamic-slice_fusion.1 = bf16[2,8,1,256,1,1,256]{6,4,5,3,2,1,0:T(2,128)(2,1)} fusion(bf16[2,8,1,256,2,1,256]{6,4,5,3,2,1,0:T(2,128)(2,1)} %param.13, s32[]{:T(128)} %select_n.170), kind=kLoop, calls=%fused_computation.180 | loop fusion | bytes 4194308 | tf_op jit(solution)/shard_map/jit(dynamic_index_in_dim)/dynamic_slice | solution.py:86
  22.9 2.7 copy.51
  25.8 1.4 and_and_fusion.2
  27.2 69.0 %all-reduce.13.cloned.1.call-done = (bf16[2,256,256]{2,1,0:T(8,128)(2,1)}, bf16[2,256,2,256]{3,1,2,0:T(8,128)(2,1)}) async-done(((bf16[2,256,256]{2,1,0:T(8,128)(2,1)}, bf16[2,256,2,256]{3,1,2,0:T(8,128)(2,1)}), (bf16[2,256,256]{2,1,0:T(8,128)(2,1)}, bf16[2,256,2,256]{3,1,2,0:T(8,128)(2,1)})) %all-reduce.13.cloned.1.call-update) | async-done | bytes 786448 | tf_op jit(solution)/shard_map/psum | solution.py:9
  96.2 1.5 broadcast_select_fusion.1
  98.0 5.0 %copy.50 = bf16[2,8,1,256,2,1,256]{6,3,4,1,0,5,2:T(8,128)(2,1)} copy(bf16[2,8,1,256,2,1,256]{6,4,5,3,2,1,0:T(2,128)(2,1)} %param.13) | data formatting | bytes 8388608 | tf_op args[0]
  106.8 113.3 %all-reduce.7.cloned.1.call-done = bf16[2,8,256,256]{3,2,1,0:T(8,128)(2,1)} async-done(((bf16[2,8,256,256]{3,2,1,0:T(8,128)(2,1)}), bf16[2,8,256,256]{3,2,1,0:T(8,128)(2,1)}) %all-reduce.7.cloned.1.call-update) | async-done | bytes 2097168 | tf_op jit(solution)/shard_map/psum | solution.py:9
  220.2 2.1 fusion.114
  223.3 1.5 copy-done
  224.8 1.2 bitcast_dynamic-update-slice_fusion.1
  225.9 0.8 fusion.112
  226.8 0.8 fusion.113
  227.7 2.6 pad_maximum_fusion.2
  230.3 0.9 select_bitcast_fusion
  231.2 0.7 broadcast_select_fusion.2
  232.0 1.7 fusion.109
  233.7 72.3 %all-reduce.11.cloned.1.call-done = (bf16[2,256,256]{2,1,0:T(8,128)(2,1)}, bf16[2,256,2,256]{3,1,2,0:T(8,128)(2,1)}) async-done(((bf16[2,256,256]{2,1,0:T(8,128)(2,1)}, bf16[2,256,2,256]{3,1,2,0:T(8,128)(2,1)}), (bf16[2,256,256]{2,1,0:T(8,128)(2,1)}, bf16[2,256,2,256]{3,1,2,0:T(8,128)(2,1)})) %all-reduce.11.cloned.1.call-update) | async-done | bytes 786448 | tf_op jit(solution)/shard_map/psum | solution.py:9
  306.0 1.3 conditional.7
  306.0 1.3 copy.64
  307.3 1.4 broadcast_select_fusion
  308.8 1.4 and_and_fusion.1
  310.3 124.2 %all-reduce.9.cloned.1.call-done = bf16[2,8,256,256]{3,2,1,0:T(8,128)(2,1)} async-done(((bf16[2,8,256,256]{3,2,1,0:T(8,128)(2,1)}), bf16[2,8,256,256]{3,2,1,0:T(8,128)(2,1)}) %all-reduce.9.cloned.1.call-update) | async-done | bytes 2097168 | tf_op jit(solution)/shard_map/psum | solution.py:9
  434.6 2.1 fusion.117
  437.4 1.5 copy-done.3
  438.9 0.9 bitcast_dynamic-update-slice_fusion
  439.8 0.8 fusion.111
  440.6 0.8 fusion.110
  441.8 6.3 %copy.32 = bf16[2,8,1,256,2,1,256]{6,4,5,3,2,1,0:T(2,128)(2,1)} copy(bf16[2,8,1,256,2,1,256]{6,3,4,1,0,5,2:T(8,128)(2,1)S(1)} %maximum_bitcast_fusion) | data formatting | bytes 8388608 | tf_op jit(solution)/shard_map/reshape | solution.py:114
  (54 shorter events, 4.0 us)
Async XLA Ops:
  6.5 6.5 %copy-start.7 = (bf16[2,2,256,256]{3,2,1,0:T(8,128)(2,1)S(1)}, bf16[2,2,256,256]{3,2,1,0:T(8,128)(2,1)}, u32[]{:S(2)}) copy-start(bf16[2,2,256,256]{3,2,1,0:T(8,128)(2,1)} %param.14) | copy-start | bytes 1572868
  6.5 89.7 %all-reduce.13.cloned.1.call-start = ((), (), s32[]{:S(2)}) async-start(), calls=%async_computation.3 | async-start | bytes 1572864 | tf_op jit(solution)/shard_map/psum | solution.py:9
  13.8 206.3 %all-reduce.7.cloned.1.call-start = ((), (), s32[]{:S(2)}) async-start(), calls=%async_computation | async-start | bytes 4194304 | tf_op jit(solution)/shard_map/psum | solution.py:9
  22.9 2.7 copy-start.14
  97.8 208.2 %all-reduce.11.cloned.1.call-start = ((), (), s32[]{:S(2)}) async-start(), calls=%async_computation.2 | async-start | bytes 1572864 | tf_op jit(solution)/shard_map/psum | solution.py:9
  98.0 7.8 %copy-start.15 = (s32[2,64]{1,0:T(2,128)S(1)}, s32[2,64]{1,0:T(2,128)}, u32[]{:S(2)}) copy-start(s32[2,64]{1,0:T(2,128)} %param.17) | copy-start | bytes 1540
  98.0 122.1 %copy-start.12 = (bf16[2,256,2,256]{3,1,2,0:T(8,128)(2,1)S(1)}, bf16[2,256,2,256]{3,1,2,0:T(8,128)(2,1)}, u32[]{:S(2)}) copy-start(bf16[2,256,2,256]{3,1,2,0:T(8,128)(2,1)} %get-tuple-element.181) | copy-start | bytes 1572868
  220.2 2.1 copy-start.4
  220.2 3.1 copy-start.6
  222.3 2.5 copy-start
  222.3 2.5 copy-start.8
  226.8 3.5 copy-start.1
  227.7 2.7 copy-start.2
  231.9 202.6 %all-reduce.9.cloned.1.call-start = ((), (), s32[]{:S(2)}) async-start(), calls=%async_computation.1 | async-start | bytes 4194304 | tf_op jit(solution)/shard_map/psum | solution.py:9
  308.8 125.8 %copy-start.13 = (bf16[2,256,2,256]{3,1,2,0:T(8,128)(2,1)S(1)}, bf16[2,256,2,256]{3,1,2,0:T(8,128)(2,1)}, u32[]{:S(2)}) copy-start(bf16[2,256,2,256]{3,1,2,0:T(8,128)(2,1)} %get-tuple-element.179) | copy-start | bytes 1572868
  434.6 2.1 copy-start.5
  436.7 2.2 copy-start.3
  436.7 2.2 copy-start.10
Sparse Core Ops, SparseCore 0:
  13.9 82.2 all-reduce.12
  99.9 120.2 all-reduce.6
  232.1 73.8 all-reduce.10
  309.1 125.3 all-reduce.8
where the time goes:
time: 452 us; the launch traced here: 455 us
  waiting for transfers between devices  379 us (84%)
  local copies, waits for them, and re-layouts  30.5 us (7%)
  between operations  19 us (4%)
  other arithmetic  17 us (4%)
  matrix products  8.86 us (2%)
    psum x4, waiting for transfers between devices, spread(): return lax.psum(kept, axis)  379 us
    unnamed x30, local copies, waits for them, and re-layouts  11 us
    dynamic_slice x1, local copies, waits for them, and re-layouts, shards(): lax.dynamic_index_in_dim(panels_tiles_now, local_col, 3, keepdims=False)  9.06 us
  transfers between devices with their start and end apart: 4, of which 4 were waited for; matrix products, arithmetic and copies ran while one was open for 5% of the time, Pallas kernels for 0%

commit v1 on v0

v1 whole, which is shorter than its diff:
```python
import jax
import jax.numpy as jnp
from jax import lax
from jax.experimental import pallas as pl
from jax.experimental.pallas import tpu as pltpu
from jax.sharding import PartitionSpec as P

MESH = pl.DeviceIdType.MESH
B = 256
HALF = 128
SLAB = 32


def gather_kernel(
    piv_ref, colq, col63, rowq, row63, xbuf, ubuf, kbuf,
    other_q, picked, from_chips, other_63, xown, from_rows, uown, mine_c, other_c, picked_c, from_chips_c, kown,
    s_half, s_col, s_col63, s_all, s_row, s_row63, s_urow, s_cor, s_ccol, s_ccol63, s_krow, s_xsib, s_ksib,
    r_half, r_col, r_col63, r_all, r_row, r_row63, r_urow, r_cor, r_ccol, r_ccol63, r_krow, r_xsib, r_ksib,
):
    z = lax.axis_index("row")
    c = lax.axis_index("col")
    chip, core = c // 2, c % 2
    last_chip = chip == 15
    q = jnp.where(piv_ref[0] == 63, piv_ref[1], piv_ref[0])
    q_row, q_chip, q_core = q % 8, (q % 32) // 2, q % 2
    q_here = q_core == core
    sibling = (z, chip * 2 + 1 - core)

    def to_chip(step):
        return lax.rem(chip + step, 16)

    def to_row(step):
        return lax.rem(z + step, 8)

    def remote(src, dst, ssem, rsem, to):
        return pltpu.make_async_remote_copy(
            src_ref=src, dst_ref=dst, send_sem=ssem, recv_sem=rsem, device_id=to, device_id_type=MESH
        )

    def on_chip(p):
        return (z, p * 2 + core)

    def on_row(w):
        return (w, c)

    bar = pltpu.get_barrier_semaphore()

    def greet_chip(i, carry):
        pl.semaphore_signal(bar, inc=1, device_id=on_chip(to_chip(i)), device_id_type=MESH)
        return carry

    def greet_row(i, carry):
        pl.semaphore_signal(bar, inc=1, device_id=on_row(to_row(i)), device_id_type=MESH)
        return carry

    lax.fori_loop(1, 16, greet_chip, 0)
    lax.fori_loop(1, 8, greet_row, 0)
    pl.semaphore_signal(bar, inc=1, device_id=sibling, device_id_type=MESH)
    pl.semaphore_wait(bar, 23)

    half_q = remote(colq.at[:, 1 - core], other_q, s_half.at[0], r_half.at[0], sibling)
    half_63 = remote(col63.at[:, 0], other_63, s_half.at[1], r_half.at[1], sibling)
    half_q.start()

    @pl.when(last_chip & (core == 1))
    def _():
        half_63.start()

    def send_row(i, carry):
        w = to_row(i)
        remote(rowq.at[w], from_rows.at[z], s_row.at[i], r_row.at[z], on_row(w)).start()

        @pl.when(z == 7)
        def _():
            remote(row63.at[w], uown.at[1], s_row63.at[i], r_row63.at[0], on_row(w)).start()
        return carry

    lax.fori_loop(1, 8, send_row, 0)

    half_q.wait_recv()

    def pick(i, carry):
        picked[i] = jnp.where(q_here, colq[i, core], other_q[i])
        return carry

    lax.fori_loop(0, 16, pick, 0)

    @pl.when(last_chip & (core == 0))
    def _():
        half_63.wait_recv()

    def send_col(i, carry):
        p = to_chip(i)
        remote(picked.at[p], from_chips.at[chip], s_col.at[i], r_col.at[chip], on_chip(p)).start()

        @pl.when(last_chip & (core == 0))
        def _():
            remote(other_63.at[p], xown.at[1], s_col63.at[i], r_col63.at[0], on_chip(p)).start()

        @pl.when(last_chip & (core == 1))
        def _():
            remote(col63.at[p, 1], xown.at[1], s_col63.at[i], r_col63.at[0], on_chip(p)).start()
        return carry

    lax.fori_loop(1, 16, send_col, 0)
    from_chips[chip] = picked[chip]

    @pl.when(last_chip)
    def _():
        xown[1] = jnp.where(core == 0, other_63[15], col63[15, 1])

    from_rows[z] = rowq[z]

    @pl.when(z == 7)
    def _():
        uown[1] = row63[7]

    def wait_row(i, carry):
        w = to_row(i)
        remote(from_rows.at[w], from_rows.at[w], s_row.at[i], r_row.at[w], on_row(w)).wait_recv()
        return carry

    lax.fori_loop(1, 8, wait_row, 0)
    uown[0] = from_rows[q_row]

    @pl.when(z != 7)
    def _():
        remote(uown.at[1], uown.at[1], s_row63.at[0], r_row63.at[0], on_row(z)).wait_recv()

    q_tc = q // 32
    for a in range(2):
        for r in range(2):
            mine_c[0, a, r] = uown[a, 2 * q_tc + r]
            mine_c[1, a, r] = uown[a, 2 + r]
    cor_q = remote(mine_c.at[0, 1 - core], other_c.at[0], s_cor.at[0], r_cor.at[0], sibling)
    cor_63 = remote(mine_c.at[1, 0], other_c.at[1], s_cor.at[1], r_cor.at[1], sibling)
    cor_q.start()

    @pl.when(last_chip & (core == 1))
    def _():
        cor_63.start()

    def send_urow(i, carry):
        remote(uown, ubuf.at[z], s_urow.at[i], r_urow.at[z], on_row(to_row(i))).start()
        return carry

    lax.fori_loop(1, 8, send_urow, 0)
    ubuf[z] = uown[...]

    cor_q.wait_recv()
    picked_c[0] = jnp.where(q_here, mine_c[0, core], other_c[0])

    @pl.when(last_chip & (core == 0))
    def _():
        cor_63.wait_recv()
        kown[1] = other_c[1]

    @pl.when(last_chip & (core == 1))
    def _():
        kown[1] = mine_c[1, 1]

    def send_ccol(i, carry):
        p = to_chip(i)
        remote(picked_c.at[0], from_chips_c.at[chip], s_ccol.at[i], r_ccol.at[chip], on_chip(p)).start()

        @pl.when(last_chip)
        def _():
            remote(kown.at[1], kown.at[1], s_ccol63.at[i], r_ccol63.at[0], on_chip(p)).start()
        return carry

    lax.fori_loop(1, 16, send_ccol, 0)
    from_chips_c[chip] = picked_c[0]

    def wait_col(i, carry):
        p = to_chip(i)
        remote(from_chips.at[p], from_chips.at[p], s_col.at[i], r_col.at[p], on_chip(p)).wait_recv()
        return carry

    lax.fori_loop(1, 16, wait_col, 0)
    xown[0] = from_chips[q_chip]

    @pl.when(jnp.logical_not(last_chip))
    def _():
        remote(xown.at[1], xown.at[1], s_col63.at[0], r_col63.at[0], sibling).wait_recv()

    def send_all(i, carry):
        remote(xown, xbuf.at[core, chip], s_all.at[i], r_all.at[chip], on_chip(to_chip(i))).start()
        return carry

    lax.fori_loop(1, 16, send_all, 0)
    xbuf[core, chip] = xown[...]

    def wait_ccol(i, carry):
        p = to_chip(i)
        remote(picked_c.at[0], from_chips_c.at[p], s_ccol.at[i], r_ccol.at[p], on_chip(p)).wait_recv()
        return carry

    lax.fori_loop(1, 16, wait_ccol, 0)
    kown[0] = from_chips_c[q_chip]

    @pl.when(jnp.logical_not(last_chip))
    def _():
        remote(kown.at[1], kown.at[1], s_ccol63.at[0], r_ccol63.at[0], sibling).wait_recv()

    def send_krow(i, carry):
        remote(kown, kbuf.at[core, z], s_krow.at[i], r_krow.at[z], on_row(to_row(i))).start()
        return carry

    lax.fori_loop(1, 8, send_krow, 0)
    kbuf[core, z] = kown[...]

    for part in range(4):
        for i in range(4 * part, 4 * part + 4):
            @pl.when(chip != i)
            def _(i=i):
                remote(xown, xbuf.at[core, i], s_all.at[0], r_all.at[i], sibling).wait_recv()
        block = xbuf.at[core, pl.ds(4 * part, 4)]
        remote(block, block, s_xsib.at[part], r_xsib.at[part], sibling).start()

    def wait_krow(i, carry):
        w = to_row(i)
        remote(kown, kbuf.at[core, w], s_krow.at[i], r_krow.at[w], on_row(w)).wait_recv()
        return carry

    lax.fori_loop(1, 8, wait_krow, 0)
    both = remote(kbuf.at[core], kbuf.at[core], s_ksib.at[0], r_ksib.at[0], sibling)
    both.start()

    def wait_urow(i, carry):
        w = to_row(i)
        remote(uown, ubuf.at[w], s_urow.at[i], r_urow.at[w], on_row(w)).wait_recv()
        return carry

    lax.fori_loop(1, 8, wait_urow, 0)

    half_q.wait_send()
    cor_q.wait_send()

    @pl.when(last_chip & (core == 1))
    def _():
        half_63.wait_send()
        cor_63.wait_send()

    def sent_rows(i, carry):
        to = on_row(to_row(i))
        remote(rowq.at[0], from_rows.at[0], s_row.at[i], r_row.at[0], to).wait_send()
        remote(uown, ubuf.at[0], s_urow.at[i], r_urow.at[0], to).wait_send()
        remote(kown, kbuf.at[0, 0], s_krow.at[i], r_krow.at[0], to).wait_send()

        @pl.when(z == 7)
        def _():
            remote(row63.at[0], uown.at[1], s_row63.at[i], r_row63.at[0], to).wait_send()
        return carry

    lax.fori_loop(1, 8, sent_rows, 0)

    def sent_chips(i, carry):
        to = on_chip(to_chip(i))
        remote(picked.at[0], from_chips.at[0], s_col.at[i], r_col.at[0], to).wait_send()
        remote(xown, xbuf.at[0, 0], s_all.at[i], r_all.at[0], to).wait_send()
        remote(picked_c.at[0], from_chips_c.at[0], s_ccol.at[i], r_ccol.at[0], to).wait_send()

        @pl.when(last_chip)
        def _():
            remote(picked.at[0], xown.at[1], s_col63.at[i], r_col63.at[0], to).wait_send()
            remote(kown.at[1], kown.at[1], s_ccol63.at[i], r_ccol63.at[0], to).wait_send()
        return carry

    lax.fori_loop(1, 16, sent_chips, 0)
    for part in range(4):
        block = xbuf.at[1 - core, pl.ds(4 * part, 4)]
        remote(block, block, s_xsib.at[part], r_xsib.at[part], sibling).wait()
    both.wait_send()
    remote(kbuf.at[1 - core], kbuf.at[1 - core], s_ksib.at[0], r_ksib.at[0], sibling).wait_recv()


def gather(pivots, colq, col63, rowq, row63):
    bf = jnp.bfloat16
    shape = jax.ShapeDtypeStruct
    vmem = pl.BlockSpec(memory_space=pltpu.VMEM)
    dma = pltpu.SemaphoreType.DMA
    sems = [dma((n,)) for n in (2, 16, 16, 16, 8, 8, 8, 2, 16, 16, 8, 4, 1)]
    return pl.pallas_call(
        gather_kernel,
        name="gather_0",
        out_shape=[
            shape((2, 16, 2, HALF, B), bf),
            shape((8, 2, 4, SLAB, B), bf),
            shape((2, 8, 2, 2, SLAB, B), bf),
        ],
        in_specs=[pl.BlockSpec(memory_space=pltpu.SMEM)] + [vmem] * 4,
        out_specs=[vmem] * 3,
        scratch_shapes=[
            pltpu.VMEM((16, HALF, B), bf), pltpu.VMEM((16, HALF, B), bf), pltpu.VMEM((16, HALF, B), bf),
            pltpu.VMEM((16, HALF, B), bf), pltpu.VMEM((2, HALF, B), bf),
            pltpu.VMEM((8, 4, SLAB, B), bf), pltpu.VMEM((2, 4, SLAB, B), bf),
            pltpu.VMEM((2, 2, 2, SLAB, B), bf), pltpu.VMEM((2, 2, SLAB, B), bf),
            pltpu.VMEM((1, 2, SLAB, B), bf), pltpu.VMEM((16, 2, SLAB, B), bf), pltpu.VMEM((2, 2, SLAB, B), bf),
        ] + sems + sems,
        compiler_params=pltpu.CompilerParams(collective_id=0, has_side_effects=True, vmem_limit_bytes=24 * 2**20),
    )(pivots, colq, col63, rowq, row63)


def split_kernel(piv_ref, m_ref, d_ref, colq_ref, col63_ref, rowq_ref, row63_ref):
    group = pl.program_id(0)
    other = jnp.where(piv_ref[0] == 63, piv_ref[1], piv_ref[0])
    out_row = lax.broadcasted_iota(jnp.int32, (B, B), 0)
    in_row = lax.broadcasted_iota(jnp.int32, (B, B), 1)
    perm = jnp.where(in_row == (out_row % 64) * 4 + out_row // 64, 1.0, 0.0).astype(jnp.bfloat16)
    for r in range(2):
        for t in range(2):
            j = 2 * r + t
            for half in range(2):
                pair = jnp.concatenate([m_ref[r, t, pl.ds((2 * half + s) * B, B), :] for s in range(2)], axis=1)
                sorted_rows = jnp.dot(perm, pair, preferred_element_type=jnp.float32).astype(jnp.bfloat16)
                for s in range(2):
                    for lb in range(2):
                        for tc in range(2):
                            piece = sorted_rows[(lb * 2 + tc) * 64:(lb * 2 + tc + 1) * 64, s * 128:(s + 1) * 128]
                            here = (pl.ds((2 * half + s) * 64, 64), pl.ds(lb * 128, 128))
                            d_ref[(tc, group, j, *here)] = piece

            for h in range(2):
                rows = pl.ds(h * HALF, HALF)
                colq_ref[8 * r + 2 * group + t, h] = d_ref[other // 32, group, j, rows]
                col63_ref[8 * r + 2 * group + t, h] = d_ref[1, group, j, rows]

            @pl.when(other // 8 == 2 * group + t)
            def _(r=r, j=j):
                for tc in range(2):
                    for w in range(8):
                        rowq_ref[w, 2 * tc + r] = d_ref[tc, group, j, pl.ds(w * SLAB, SLAB)]

            if t == 1:
                @pl.when(group == 3)
                def _(r=r, j=j):
                    for tc in range(2):
                        for w in range(8):
                            row63_ref[w, 2 * tc + r] = d_ref[tc, group, j, pl.ds(w * SLAB, SLAB)]


def split(pivots, packed):
    shape = jax.ShapeDtypeStruct
    vmem = pl.BlockSpec(memory_space=pltpu.VMEM)
    return pl.pallas_call(
        split_kernel,
        name="split",
        grid=(4,),
        out_shape=[
            shape((2, 4, 4, B, B), jnp.bfloat16),
            shape((16, 2, HALF, B), jnp.bfloat16),
            shape((16, 2, HALF, B), jnp.bfloat16),
            shape((8, 4, SLAB, B), jnp.bfloat16),
            shape((8, 4, SLAB, B), jnp.bfloat16),
        ],
        in_specs=[
            pl.BlockSpec(memory_space=pltpu.SMEM),
            pl.BlockSpec((2, 2, 4 * B, 128), lambda g: (0, g, 0, 0)),
        ],
        out_specs=[vmem] * 5,
        compiler_params=pltpu.CompilerParams(vmem_limit_bytes=24 * 2**20),
    )(pivots, packed)


def dot(left, right):
    return jnp.dot(left, right, preferred_element_type=jnp.float32)


def flat(pair):
    return jnp.concatenate([pair[0], pair[1]], axis=1)


def store_right(ref, pair, at=0, width=B):
    ref[pl.ds(0, B), pl.ds(at, B)] = pair[0]
    ref[pl.ds(B, B), pl.ds(at, B)] = -pair[1]
    ref[pl.ds(0, B), pl.ds(at + width, B)] = pair[1]
    ref[pl.ds(B, B), pl.ds(at + width, B)] = pair[0]


def halves(wide):
    return wide[:, :B], wide[:, B:]


def update_kernel(
    piv_ref, cl_ref, rl_ref, inv_ref, x_ref, u_ref, k_ref, d_ref, o_ref,
    f0, f1, rx0, rx1, rm01, ru0, ru1, tmp, l0, l1, tile,
):
    bf, f32 = jnp.bfloat16, jnp.float32
    group = pl.program_id(0)
    z = lax.axis_index("row")
    c = lax.axis_index("col")
    p0, p1 = piv_ref[0], piv_ref[1]
    s0 = jnp.where(p0 == 63, 1, 0)
    s1 = 1 - s0
    col_ids = [tc * 32 + c for tc in range(2)]
    cols0 = [(rl_ref[0, i] > 0) & (i != p0) for i in col_ids]
    cols1 = [(rl_ref[1, i] > 0) & (i != p0) & (i != p1) for i in col_ids]

    def from_column(s, r, row):
        return jnp.concatenate([x_ref[h, 8 * r + row, s] for h in range(2)], axis=0)

    def from_row(s, at):
        return jnp.concatenate([u_ref[w, s, at] for w in range(8)], axis=0)

    def corner(row, col):
        return [jnp.concatenate([k_ref[row, w, col, r] for w in range(8)], axis=0) for r in range(2)]

    def taken(row):
        return (cl_ref[0, row] > 0) & (row != p0), (cl_ref[1, row] > 0) & (row != p0) & (row != p1)

    @pl.when(group == 0)
    def _():
        def refine(diagonal, step, keep, keep_right):
            guess = (inv_ref[step, 0], inv_ref[step, 1])
            store_right(tmp, guess)
            eye = lax.broadcasted_iota(jnp.int32, (B, B), 0) == lax.broadcasted_iota(jnp.int32, (B, B), 1)
            real, imag = halves(dot(diagonal, tmp[...]))
            store_right(tmp, ((jnp.where(eye, 2.0, 0.0) - real).astype(bf), (-imag).astype(bf)))
            keep[...] = dot(flat(guess), tmp[...]).astype(bf)
            store_right(keep_right, halves(keep[...]))

        refine(flat(corner(s0, s0)), 0, f0, rx0)
        l10 = dot(flat(corner(s1, s0)), rx0[...]).astype(bf)
        store_right(rm01, corner(s0, s1))
        m11 = (flat(corner(s1, s1)).astype(f32) - dot(l10, rm01[...])).astype(bf)
        refine(m11, 1, f1, rx1)
        for tc in range(2):
            store_right(ru0, (from_row(s0, 2 * tc), from_row(s0, 2 * tc + 1)), tc * B, 2 * B)
        product = dot(l10, ru0[...])
        for tc in range(2):
            pair = []
            for r in range(2):
                old = from_row(s1, 2 * tc + r).astype(f32)
                at = (2 * r + tc) * B
                pair.append(jnp.where(cols0[tc], old - product[:, at:at + B], old).astype(bf))
            store_right(ru1, pair, tc * B, 2 * B)
        for q in range(4):
            flags = [taken((2 * q + t) * 8 + z) for t in range(2)]
            rows = [pl.ds((2 * q + t) * B, B) for t in range(2)]
            both = pl.ds(2 * q * B, 2 * B)

            def panel(s, q=q):
                return jnp.concatenate([flat([from_column(s, r, 2 * q + t) for r in range(2)]) for t in range(2)], axis=0)

            def mixed(product, old, which):
                return jnp.concatenate(
                    [
                        jnp.where(flags[t][which], product[t * B:(t + 1) * B], old[t * B:(t + 1) * B])
                        for t in range(2)
                    ],
                    axis=0,
                ).astype(bf)

            old = panel(s0)
            left = mixed(dot(old, rx0[...]), old.astype(f32), 0)
            l0[both, :] = left
            old = panel(s1).astype(f32)
            moved = mixed(old - dot(left, rm01[...]), old, 0)
            l1[both, :] = mixed(dot(moved, rx1[...]), moved.astype(f32), 1)

    first = dot(l0[pl.ds(2 * group * B, 2 * B), :], ru0[...])
    second = dot(l1[pl.ds(2 * group * B, 2 * B), :], ru1[...])
    for t in range(2):
        take0, take1 = taken((2 * group + t) * 8 + z)
        for tc in range(2):
            use0 = take0 & cols0[tc] & (col_ids[tc] != p1)
            use1 = take1 & cols1[tc]
            for r in range(2):
                old = d_ref[tc, group, 2 * r + t].astype(f32)
                at = (2 * r + tc) * B
                rows = slice(t * B, (t + 1) * B)
                old = jnp.where(use0, old - first[rows, at:at + B], old).astype(bf).astype(f32)
                tile[t, tc, r] = jnp.where(use1, old - second[rows, at:at + B], old).astype(bf)

    for tc in range(2):
        for pivot, left, factor in ((p0, l0, f0), (p1, l1, f1)):
            @pl.when(col_ids[tc] == pivot)
            def _(tc=tc, pivot=pivot, left=left, factor=factor):
                for t in range(2):
                    is_pivot = (2 * group + t) * 8 + z == pivot
                    for r in range(2):
                        lanes = pl.ds(r * B, B)
                        other = left[pl.ds((2 * group + t) * B, B), lanes].astype(f32)
                        tile[t, tc, r] = jnp.where(is_pivot, factor[:, lanes].astype(f32), other).astype(bf)

    out_row = lax.broadcasted_iota(jnp.int32, (B, B), 0)
    in_row = lax.broadcasted_iota(jnp.int32, (B, B), 1)
    perm = jnp.where(out_row == (in_row % 64) * 4 + in_row // 64, 1.0, 0.0).astype(bf)
    for t in range(2):
        for r in range(2):
            for half in range(2):
                stacked = jnp.concatenate(
                    [
                        jnp.concatenate(
                            [tile[t, tc, r, pl.ds((2 * half + s) * 64, 64), pl.ds(lb * 128, 128)] for s in range(2)],
                            axis=1,
                        )
                        for lb in range(2)
                        for tc in range(2)
                    ],
                    axis=0,
                )
                woven = dot(perm, stacked).astype(bf)
                for s in range(2):
                    o_ref[r, t, pl.ds((2 * half + s) * B, B), :] = woven[:, s * 128:(s + 1) * 128]


def update(pivots, col_lists, row_lists, inverses, x, u, k, d):
    smem = pl.BlockSpec(memory_space=pltpu.SMEM)
    vmem_in = pl.BlockSpec(memory_space=pltpu.VMEM)
    square = pltpu.VMEM((2 * B, 2 * B), jnp.bfloat16)
    flat_square = pltpu.VMEM((B, 2 * B), jnp.bfloat16)
    wide = pltpu.VMEM((2 * B, 4 * B), jnp.bfloat16)
    panel = pltpu.VMEM((8 * B, 2 * B), jnp.bfloat16)
    return pl.pallas_call(
        update_kernel,
        name="update",
        grid=(4,),
        out_shape=jax.ShapeDtypeStruct((2, 8, 4 * B, 128), jnp.bfloat16),
        in_specs=[smem] * 3 + [vmem_in] * 5,
        out_specs=pl.BlockSpec((2, 2, 4 * B, 128), lambda g: (0, g, 0, 0)),
        scratch_shapes=[
            flat_square, flat_square, square, square, square, wide, wide, square, panel, panel,
            pltpu.VMEM((2, 2, 2, B, B), jnp.bfloat16),
        ],
        compiler_params=pltpu.CompilerParams(vmem_limit_bytes=32 * 2**20),
    )(pivots, col_lists, row_lists, inverses, x, u, k, d)


def shards(matrix, inverses, pivots, col_lists, row_lists):
    packed = matrix.reshape(2, 8, B, 2, 2, 128).transpose(0, 1, 2, 4, 3, 5).reshape(2, 8, 4 * B, 128)
    d, colq, col63, rowq, row63 = split(pivots, packed)
    x, u, k = gather(pivots, colq, col63, rowq, row63)
    out = update(pivots, col_lists, row_lists, inverses, x, u, k, d)
    return out.reshape(2, 8, B, 2, 2, 128).transpose(0, 1, 2, 4, 3, 5).reshape(matrix.shape)


def solution(mesh):
    tiled = P(None, None, "row", None, None, "col", None)
    return jax.shard_map(shards, mesh=mesh, in_specs=(tiled, P(), P(), P(), P()), out_specs=tiled, check_vma=False)
```

time: 452 us -> 102 us (0.23)
  the two profiles are of different devices: /device:TPU:1 before, /device:TPU:193 now
where the time goes in v1:
time: 102 us; the launch traced here: 101 us
  Pallas kernels  98.5 us (97%)
  local copies, waits for them, and re-layouts  2.86 us (3%)
    pallas_call x1, Pallas kernels, gather(): pl.pallas_call(gather_kernel, name='gather_0', out_shape=[shape((2, 16, 2...  79.3 us
    pallas_call x1, Pallas kernels, update(): pl.pallas_call(update_kernel, name='update', grid=(4,), out_shape=jax.Sha...  14.2 us
    pallas_call x1, Pallas kernels, split(): pl.pallas_call(split_kernel, name='split', grid=(4,), out_shape=[shape((2...  5.05 us
    unnamed x12, local copies, waits for them, and re-layouts  2.86 us

profile of v1, /device:TPU:193, one launch (start us, length us, event | category | flops | bytes accessed | tf_op | source)
XLA Modules:
  0.0 101.4 jit_solution(7921281785111279833)
XLA Ops:
  0.0 0.0 copy-start
  0.0 2.2 %copy-done = bf16[2,8,1,256,2,1,256]{6,4,5,3,2,1,0:T(2,128)(2,1)S(1)} copy-done((bf16[2,8,1,256,2,1,256]{6,4,5,3,2,1,0:T(2,128)(2,1)S(1)}, bf16[2,8,1,256,2,1,256]{6,4,5,3,2,1,0:T(2,128)(2,1)}, u32[]{:S(2)}) %copy-start) | copy-done | bytes 4194328
  2.2 0.0 copy-start.2
  2.2 0.7 copy-done.2
  2.8 0.0 copy-start.1
  2.8 0.0 copy-start.3
  2.8 0.0 copy-start.4
  2.9 0.0 copy-start.5
  2.9 5.0 %split.1 = (bf16[2,4,4,256,256]{4,3,2,1,0:T(8,128)(2,1)S(1)}, bf16[16,2,128,256]{3,2,1,0:T(8,128)(2,1)S(1)}, bf16[16,2,128,256]{3,2,1,0:T(8,128)(2,1)S(1)}, bf16...) custom-call(s32[2]{0:T(128)S(1)} %copy-done.2, bf16[2,8,1024,128]{3,2,1,0:T(8,128)(2,1)S(1)} %bitcast.10), custom_call_target="tpu_custom_call" | custom-call | tf_op jit(solution)/shard_map/split/pallas_call | solution.py:345
  7.9 79.3 %gather_0.1 = (bf16[2,16,2,128,256]{4,3,2,1,0:T(8,128)(2,1)S(1)}, bf16[8,2,4,32,256]{4,3,2,1,0:T(8,128)(2,1)S(1)}, bf16[2,8,2,2,32,256]{5,4,3,2,1,0:T(8,128)(2,1)S(1)}) custom-call(s32[2]{0:T(128)S(1)} %copy-done.2, bf16[16,2,128,256]{3,2,1,0:T(8,128)(2,1)S(1)} %get-tuple-element.13.colq, bf16[16,2,128,256]{3,2,1,0:T(8,128)(2,1)S(1)} %get-tuple-element.14.col63, ...), custom_call_target="tpu_custom_call" | custom-call | tf_op jit(solution)/shard_map/gather_0/pallas_call | solution.py:283
  87.2 0.0 copy-done.1
  87.2 0.0 copy-done.3
  87.2 0.0 copy-done.4
  87.2 0.0 copy-done.5
  87.2 14.2 %update.1 = bf16[2,8,1024,128]{3,2,1,0:T(8,128)(2,1)} custom-call(s32[2]{0:T(128)S(1)} %copy-done.3, s32[2,64]{1,0:T(2,128)S(1)} %copy-done.4, s32[2,64]{1,0:T(2,128)S(1)} %copy-done.5, bf16[2,2,256,256]{3,2,1,0:T(8,128)(2,1)S(1)} %copy-done.1, bf16[2,16,2,128,256]{4,3,2,1,0:T(8,128)(2,1)S(1)} %get-tuple-element.17.x_ref, ...), custom_call_target="tpu_custom_call" | custom-call | tf_op jit(solution)/shard_map/update/pallas_call | solution.py:515
Async XLA Ops:
  0.0 2.2 %copy-start = (bf16[2,8,1,256,2,1,256]{6,4,5,3,2,1,0:T(2,128)(2,1)S(1)}, bf16[2,8,1,256,2,1,256]{6,4,5,3,2,1,0:T(2,128)(2,1)}, u32[]{:S(2)}) copy-start(bf16[2,8,1,256,2,1,256]{6,4,5,3,2,1,0:T(2,128)(2,1)} %param.5) | copy-start | bytes 12582916
  2.2 0.7 copy-start.2
  2.8 84.4 %copy-start.1 = (bf16[2,2,256,256]{3,2,1,0:T(8,128)(2,1)S(1)}, bf16[2,2,256,256]{3,2,1,0:T(8,128)(2,1)}, u32[]{:S(2)}) copy-start(bf16[2,2,256,256]{3,2,1,0:T(8,128)(2,1)} %inv_ref.1) | copy-start | bytes 1572868
  2.8 84.4 %copy-start.3 = (s32[2]{0:T(128)S(1)}, s32[2]{0:T(128)}, u32[]{:S(2)}) copy-start(s32[2]{0:T(128)} %piv_ref.5) | copy-start | bytes 28
  2.8 84.4 %copy-start.4 = (s32[2,64]{1,0:T(2,128)S(1)}, s32[2,64]{1,0:T(2,128)}, u32[]{:S(2)}) copy-start(s32[2,64]{1,0:T(2,128)} %cl_ref.1) | copy-start | bytes 1540
  2.9 84.4 %copy-start.5 = (s32[2,64]{1,0:T(2,128)S(1)}, s32[2,64]{1,0:T(2,128)}, u32[]{:S(2)}) copy-start(s32[2,64]{1,0:T(2,128)} %rl_ref.1) | copy-start | bytes 1540

commit v2 on v1

--- a/solution.py
+++ b/solution.py
@@ -13,9 +13,9 @@
 
 def gather_kernel(
     piv_ref, colq, col63, rowq, row63, xbuf, ubuf, kbuf,
-    other_q, picked, from_chips, other_63, xown, from_rows, uown, mine_c, other_c, picked_c, from_chips_c, kown,
-    s_half, s_col, s_col63, s_all, s_row, s_row63, s_urow, s_cor, s_ccol, s_ccol63, s_krow, s_xsib, s_ksib,
-    r_half, r_col, r_col63, r_all, r_row, r_row63, r_urow, r_cor, r_ccol, r_ccol63, r_krow, r_xsib, r_ksib,
+    other_q, picked, from_chips, other_63, xown, from_rows, uown, mine_c, other_c, from_x, picked_c, from_y, kown,
+    s_half, s_col, s_col63, s_ax, s_ay, s_row, s_row63, s_urow, s_cor, s_cx, s_cy, s_krow, s_xsib, s_ksib,
+    r_half, r_col, r_col63, r_ax, r_ay, r_row, r_row63, r_urow, r_cor, r_cx, r_cy, r_krow, r_xsib, r_ksib,
 ):
     z = lax.axis_index("row")
     c = lax.axis_index("col")
@@ -24,6 +24,7 @@
     q = jnp.where(piv_ref[0] == 63, piv_ref[1], piv_ref[0])
     q_row, q_chip, q_core = q % 8, (q % 32) // 2, q % 2
     q_here = q_core == core
+    cx, cy = chip % 4, chip // 4
     sibling = (z, chip * 2 + 1 - core)
 
     def to_chip(step):
@@ -43,6 +44,18 @@
     def on_row(w):
         return (w, c)
 
+    def x_mate(i):
+        return lax.rem(cx + i, 4)
+
+    def y_mate(i):
+        return lax.rem(cy + i, 4)
+
+    def on_x(v):
+        return on_chip(cy * 4 + v)
+
+    def on_y(v):
+        return on_chip(v * 4 + cx)
+
     bar = pltpu.get_barrier_semaphore()
 
     def greet_chip(i, carry):
@@ -77,6 +90,26 @@
 
     lax.fori_loop(1, 8, send_row, 0)
 
+    @pl.when(last_chip & (core == 0))
+    def _():
+        half_63.wait_recv()
+
+    @pl.when(last_chip)
+    def _():
+        def send_63(i, carry):
+            p = to_chip(i)
+
+            @pl.when(core == 0)
+            def _():
+                remote(other_63.at[p], xown.at[1], s_col63.at[i], r_col63.at[0], on_chip(p)).start()
+
+            @pl.when(core == 1)
+            def _():
+                remote(col63.at[p, 1], xown.at[1], s_col63.at[i], r_col63.at[0], on_chip(p)).start()
+            return carry
+
+        lax.fori_loop(1, 16, send_63, 0)
+
     half_q.wait_recv()
 
     def pick(i, carry):
@@ -84,22 +117,10 @@
         return carry
 
     lax.fori_loop(0, 16, pick, 0)
-
-    @pl.when(last_chip & (core == 0))
-    def _():
-        half_63.wait_recv()
 
     def send_col(i, carry):
         p = to_chip(i)
         remote(picked.at[p], from_chips.at[chip], s_col.at[i], r_col.at[chip], on_chip(p)).start()
-
-        @pl.when(last_chip & (core == 0))
-        def _():
-            remote(other_63.at[p], xown.at[1], s_col63.at[i], r_col63.at[0], on_chip(p)).start()
-
-        @pl.when(last_chip & (core == 1))
-        def _():
-            remote(col63.at[p, 1], xown.at[1], s_col63.at[i], r_col63.at[0], on_chip(p)).start()
         return carry
 
     lax.fori_loop(1, 16, send_col, 0)
@@ -130,46 +151,114 @@
     q_tc = q // 32
     for a in range(2):
         for r in range(2):
-            mine_c[0, a, r] = uown[a, 2 * q_tc + r]
-            mine_c[1, a, r] = uown[a, 2 + r]
-    cor_q = remote(mine_c.at[0, 1 - core], other_c.at[0], s_cor.at[0], r_cor.at[0], sibling)
-    cor_63 = remote(mine_c.at[1, 0], other_c.at[1], s_cor.at[1], r_cor.at[1], sibling)
-    cor_q.start()
-
-    @pl.when(last_chip & (core == 1))
-    def _():
-        cor_63.start()
-
-    def send_urow(i, carry):
-        remote(uown, ubuf.at[z], s_urow.at[i], r_urow.at[z], on_row(to_row(i))).start()
-        return carry
-
-    lax.fori_loop(1, 8, send_urow, 0)
+            mine_c[a, 0, r] = uown[a, 2 * q_tc + r]
+            mine_c[a, 1, r] = uown[a, 2 + r]
+    cor = remote(mine_c.at[1 - core], other_c, s_cor.at[0], r_cor.at[0], sibling)
+    cor.start()
+
+    def line_send(line, src):
+        view, ssem, rsem, me, mate, on = line
+        for i in (1, 3):
+            remote(src, view(me), ssem.at[i], rsem.at[me], on(mate(i))).start()
+
+    def line_pass(line):
+        view, ssem, rsem, me, mate, on = line
+        for i, half in ((3, 0), (1, 1)):
+            v = mate(i)
+            remote(view(v), view(v), ssem.at[i], rsem.at[v], on(v)).wait_recv()
+            part = view(v, half)
+            remote(part, part, ssem.at[2 * half], rsem.at[4 + half], on(mate(4 - i))).start()
+
+    def line_end(line):
+        view, ssem, rsem, me, mate, on = line
+        for half in range(2):
+            part = view(mate(2), half)
+            remote(part, part, ssem.at[2 * half], rsem.at[4 + half], on(mate(2))).wait_recv()
+
+    def line_sent(line, src):
+        view, ssem, rsem, me, mate, on = line
+        for i in (1, 3):
+            remote(src, src, ssem.at[i], rsem.at[0], on(mate(i))).wait_send()
+        for half in range(2):
+            part = view(me, half)
+            remote(part, part, ssem.at[2 * half], rsem.at[0], on(mate(1))).wait_send()
+
+    def rows_of(half):
+        return pl.ds(0, HALF) if half is None else pl.ds(half * (HALF // 2), HALF // 2)
+
+    def y_unit(v, half=None):
+        return xbuf.at[1, core, v, cx, rows_of(half)]
+
+    def x_lines(v, half=None):
+        return xbuf.at[1, core, :, v, rows_of(half)]
+
+    def x_unit(v, half=None):
+        return xbuf.at[0, core, cy, v, rows_of(half)]
+
+    def y_lines(v, half=None):
+        return xbuf.at[0, core, v, :, rows_of(half)]
+
+    line_63y = (y_unit, s_ay.at[1], r_ay.at[1], cy, y_mate, on_y)
+    line_63x = (x_lines, s_ax.at[1], r_ax.at[1], cx, x_mate, on_x)
+    line_qx = (x_unit, s_ax.at[0], r_ax.at[0], cx, x_mate, on_x)
+    line_qy = (y_lines, s_ay.at[0], r_ay.at[0], cy, y_mate, on_y)
+
+    def ring_send(ring, src):
+        view, ssem, rsem = ring
+        remote(src, view(z), ssem.at[0], rsem.at[z], on_row(to_row(1))).start()
+        remote(src, view(z), ssem.at[4], rsem.at[z], on_row(to_row(7))).start()
+
+    def ring_pass(ring, step):
+        view, ssem, rsem = ring
+        part = view(to_row(8 - step))
+        remote(part, part, ssem.at[0], rsem.at[to_row(8 - step)], on_row(z)).wait_recv()
+        if step < 4:
+            remote(part, part, ssem.at[step], rsem.at[to_row(8 - step)], on_row(to_row(1))).start()
+            part = view(to_row(step))
+            remote(part, part, ssem.at[4], rsem.at[to_row(step)], on_row(z)).wait_recv()
+        if step < 3:
+            remote(part, part, ssem.at[4 + step], rsem.at[to_row(step)], on_row(to_row(7))).start()
+
+    def ring_sent(ring):
+        view, ssem, rsem = ring
+        for i in range(7):
+            remote(view(0), view(0), ssem.at[i], rsem.at[0], on_row(z)).wait_send()
+
+    ring_u = (lambda w: ubuf.at[w], s_urow, r_urow)
+    ring_k = (lambda w: kbuf.at[core, w], s_krow, r_krow)
+
+    cor.wait_recv()
+    for b, here in ((0, q_here), (1, core == 1)):
+        from_x[cx, b] = jnp.where(here, mine_c[core, b], other_c[b])
+    for i in range(1, 4):
+        remote(from_x.at[cx], from_x.at[cx], s_cx.at[i], r_cx.at[cx], on_x(x_mate(i))).start()
+    ring_send(ring_u, uown)
     ubuf[z] = uown[...]
-
-    cor_q.wait_recv()
-    picked_c[0] = jnp.where(q_here, mine_c[0, core], other_c[0])
-
-    @pl.when(last_chip & (core == 0))
-    def _():
-        cor_63.wait_recv()
-        kown[1] = other_c[1]
-
-    @pl.when(last_chip & (core == 1))
-    def _():
-        kown[1] = mine_c[1, 1]
-
-    def send_ccol(i, carry):
-        p = to_chip(i)
-        remote(picked_c.at[0], from_chips_c.at[chip], s_ccol.at[i], r_ccol.at[chip], on_chip(p)).start()
-
-        @pl.when(last_chip)
-        def _():
-            remote(kown.at[1], kown.at[1], s_ccol63.at[i], r_ccol63.at[0], on_chip(p)).start()
-        return carry
-
-    lax.fori_loop(1, 16, send_ccol, 0)
-    from_chips_c[chip] = picked_c[0]
+    for i in range(1, 4):
+        v = x_mate(i)
+        remote(from_x.at[v], from_x.at[v], s_cx.at[i], r_cx.at[v], on_x(v)).wait_recv()
+    picked_c[0] = from_x[q_chip % 4, 0]
+    picked_c[1] = from_x[3, 1]
+    for i in range(1, 4):
+        remote(picked_c, from_y.at[cy], s_cy.at[i], r_cy.at[cy], on_y(y_mate(i))).start()
+    from_y[cy] = picked_c[...]
+    ring_pass(ring_u, 1)
+
+    for i in range(1, 4):
+        v = y_mate(i)
+        remote(picked_c, from_y.at[v], s_cy.at[i], r_cy.at[v], on_y(v)).wait_recv()
+    kown[0] = from_y[q_chip // 4, 0]
+    kown[1] = from_y[3, 1]
+    ring_send(ring_k, kown)
+    kbuf[core, z] = kown[...]
+
+    @pl.when(jnp.logical_not(last_chip))
+    def _():
+        remote(xown.at[1], xown.at[1], s_col63.at[0], r_col63.at[0], sibling).wait_recv()
+
+    line_send(line_63y, xown.at[1])
+    xbuf[1, core, cy, cx] = xown[1]
+    ring_pass(ring_u, 2)
 
     def wait_col(i, carry):
         p = to_chip(i)
@@ -178,74 +267,46 @@
 
     lax.fori_loop(1, 16, wait_col, 0)
     xown[0] = from_chips[q_chip]
-
-    @pl.when(jnp.logical_not(last_chip))
-    def _():
-        remote(xown.at[1], xown.at[1], s_col63.at[0], r_col63.at[0], sibling).wait_recv()
-
-    def send_all(i, carry):
-        remote(xown, xbuf.at[core, chip], s_all.at[i], r_all.at[chip], on_chip(to_chip(i))).start()
-        return carry
-
-    lax.fori_loop(1, 16, send_all, 0)
-    xbuf[core, chip] = xown[...]
-
-    def wait_ccol(i, carry):
-        p = to_chip(i)
-        remote(picked_c.at[0], from_chips_c.at[p], s_ccol.at[i], r_ccol.at[p], on_chip(p)).wait_recv()
-        return carry
-
-    lax.fori_loop(1, 16, wait_ccol, 0)
-    kown[0] = from_chips_c[q_chip]
-
-    @pl.when(jnp.logical_not(last_chip))
-    def _():
-        remote(kown.at[1], kown.at[1], s_ccol63.at[0], r_ccol63.at[0], sibling).wait_recv()
-
-    def send_krow(i, carry):
-        remote(kown, kbuf.at[core, z], s_krow.at[i], r_krow.at[z], on_row(to_row(i))).start()
-        return carry
-
-    lax.fori_loop(1, 8, send_krow, 0)
-    kbuf[core, z] = kown[...]
-
-    for part in range(4):
-        for i in range(4 * part, 4 * part + 4):
-            @pl.when(chip != i)
-            def _(i=i):
-                remote(xown, xbuf.at[core, i], s_all.at[0], r_all.at[i], sibling).wait_recv()
-        block = xbuf.at[core, pl.ds(4 * part, 4)]
-        remote(block, block, s_xsib.at[part], r_xsib.at[part], sibling).start()
-
-    def wait_krow(i, carry):
-        w = to_row(i)
-        remote(kown, kbuf.at[core, w], s_krow.at[i], r_krow.at[w], on_row(w)).wait_recv()
-        return carry
-
-    lax.fori_loop(1, 8, wait_krow, 0)
+    line_send(line_qx, xown.at[0])
+    xbuf[0, core, cy, cx] = xown[0]
+    ring_pass(ring_k, 1)
+    line_pass(line_63y)
+    line_pass(line_qx)
+    ring_pass(ring_u, 3)
+    ring_pass(ring_k, 2)
+    line_end(line_63y)
+    line_send(line_63x, x_lines(cx))
+    line_end(line_qx)
+    line_send(line_qy, y_lines(cy))
+
+    def to_sibling(part, i):
+        remote(part, part, s_xsib.at[i], r_xsib.at[i], sibling).start()
+
+    to_sibling(xbuf.at[0, core, cy], 0)
+    ring_pass(ring_k, 3)
+    ring_pass(ring_u, 4)
+    line_pass(line_63x)
+    line_pass(line_qy)
+    ring_pass(ring_k, 4)
     both = remote(kbuf.at[core], kbuf.at[core], s_ksib.at[0], r_ksib.at[0], sibling)
     both.start()
-
-    def wait_urow(i, carry):
-        w = to_row(i)
-        remote(uown, ubuf.at[w], s_urow.at[i], r_urow.at[w], on_row(w)).wait_recv()
-        return carry
-
-    lax.fori_loop(1, 8, wait_urow, 0)
+    to_sibling(xbuf.at[0, core, y_mate(1)], 1)
+    to_sibling(xbuf.at[0, core, y_mate(3)], 3)
+    line_end(line_63x)
+    to_sibling(xbuf.at[1, core], 4)
+    line_end(line_qy)
+    to_sibling(xbuf.at[0, core, y_mate(2)], 2)
 
     half_q.wait_send()
-    cor_q.wait_send()
+    cor.wait_send()
 
     @pl.when(last_chip & (core == 1))
     def _():
         half_63.wait_send()
-        cor_63.wait_send()
 
     def sent_rows(i, carry):
         to = on_row(to_row(i))
         remote(rowq.at[0], from_rows.at[0], s_row.at[i], r_row.at[0], to).wait_send()
-        remote(uown, ubuf.at[0], s_urow.at[i], r_urow.at[0], to).wait_send()
-        remote(kown, kbuf.at[0, 0], s_krow.at[i], r_krow.at[0], to).wait_send()
 
         @pl.when(z == 7)
         def _():
@@ -257,19 +318,27 @@
     def sent_chips(i, carry):
         to = on_chip(to_chip(i))
         remote(picked.at[0], from_chips.at[0], s_col.at[i], r_col.at[0], to).wait_send()
-        remote(xown, xbuf.at[0, 0], s_all.at[i], r_all.at[0], to).wait_send()
-        remote(picked_c.at[0], from_chips_c.at[0], s_ccol.at[i], r_ccol.at[0], to).wait_send()
 
         @pl.when(last_chip)
         def _():
             remote(picked.at[0], xown.at[1], s_col63.at[i], r_col63.at[0], to).wait_send()
-            remote(kown.at[1], kown.at[1], s_ccol63.at[i], r_ccol63.at[0], to).wait_send()
         return carry
 
     lax.fori_loop(1, 16, sent_chips, 0)
-    for part in range(4):
-        block = xbuf.at[1 - core, pl.ds(4 * part, 4)]
-        remote(block, block, s_xsib.at[part], r_xsib.at[part], sibling).wait()
+    ring_sent(ring_u)
+    ring_sent(ring_k)
+    line_sent(line_63y, xown.at[1])
+    line_sent(line_63x, x_lines(cx))
+    line_sent(line_qx, xown.at[0])
+    line_sent(line_qy, y_lines(cy))
+    for i in range(1, 4):
+        remote(picked_c, picked_c, s_cx.at[i], r_cx.at[0], sibling).wait_send()
+        remote(picked_c, picked_c, s_cy.at[i], r_cy.at[0], sibling).wait_send()
+    for i in range(4):
+        line = xbuf.at[0, 1 - core, y_mate(i)]
+        remote(line, line, s_xsib.at[i], r_xsib.at[i], sibling).wait()
+    whole = xbuf.at[1, 1 - core]
+    remote(whole, whole, s_xsib.at[4], r_xsib.at[4], sibling).wait()
     both.wait_send()
     remote(kbuf.at[1 - core], kbuf.at[1 - core], s_ksib.at[0], r_ksib.at[0], sibling).wait_recv()
 
@@ -279,12 +348,12 @@
     shape = jax.ShapeDtypeStruct
     vmem = pl.BlockSpec(memory_space=pltpu.VMEM)
     dma = pltpu.SemaphoreType.DMA
-    sems = [dma((n,)) for n in (2, 16, 16, 16, 8, 8, 8, 2, 16, 16, 8, 4, 1)]
+    sems = [dma(n) for n in ((2,), (16,), (16,), (2, 6), (2, 6), (8,), (8,), (8,), (1,), (4,), (4,), (8,), (5,), (1,))]
     return pl.pallas_call(
         gather_kernel,
         name="gather_0",
         out_shape=[
-            shape((2, 16, 2, HALF, B), bf),
+            shape((2, 2, 4, 4, HALF, B), bf),
             shape((8, 2, 4, SLAB, B), bf),
             shape((2, 8, 2, 2, SLAB, B), bf),
         ],
@@ -295,7 +364,8 @@
             pltpu.VMEM((16, HALF, B), bf), pltpu.VMEM((2, HALF, B), bf),
             pltpu.VMEM((8, 4, SLAB, B), bf), pltpu.VMEM((2, 4, SLAB, B), bf),
             pltpu.VMEM((2, 2, 2, SLAB, B), bf), pltpu.VMEM((2, 2, SLAB, B), bf),
-            pltpu.VMEM((1, 2, SLAB, B), bf), pltpu.VMEM((16, 2, SLAB, B), bf), pltpu.VMEM((2, 2, SLAB, B), bf),
+            pltpu.VMEM((4, 2, 2, SLAB, B), bf), pltpu.VMEM((2, 2, SLAB, B), bf),
+            pltpu.VMEM((4, 2, 2, SLAB, B), bf), pltpu.VMEM((2, 2, SLAB, B), bf),
         ] + sems + sems,
         compiler_params=pltpu.CompilerParams(collective_id=0, has_side_effects=True, vmem_limit_bytes=24 * 2**20),
     )(pivots, colq, col63, rowq, row63)
@@ -397,7 +467,7 @@
     cols1 = [(rl_ref[1, i] > 0) & (i != p0) & (i != p1) for i in col_ids]
 
     def from_column(s, r, row):
-        return jnp.concatenate([x_ref[h, 8 * r + row, s] for h in range(2)], axis=0)
+        return jnp.concatenate([x_ref[s, h, 2 * r + row // 4, row % 4] for h in range(2)], axis=0)
 
     def from_row(s, at):
         return jnp.concatenate([u_ref[w, s, at] for w in range(8)], axis=0)

time: 102 us -> 89.2 us (0.87)
  the two profiles are of different devices: /device:TPU:193 before, /device:TPU:1 now
where the time goes in v2:
time: 89.2 us; the launch traced here: 89.1 us
  Pallas kernels  86.2 us (97%)
  local copies, waits for them, and re-layouts  2.86 us (3%)
    pallas_call x1, Pallas kernels, gather(): pl.pallas_call(gather_kernel, name='gather_0', out_shape=[shape((2, 2, 4,...  66.9 us
    pallas_call x1, Pallas kernels, update(): pl.pallas_call(update_kernel, name='update', grid=(4,), out_shape=jax.Sha...  14.2 us
    pallas_call x1, Pallas kernels, split(): pl.pallas_call(split_kernel, name='split', grid=(4,), out_shape=[shape((2...  5.07 us
    unnamed x12, local copies, waits for them, and re-layouts  2.86 us

profile of v2, /device:TPU:1, one launch (start us, length us, event | category | flops | bytes accessed | tf_op | source)
XLA Modules:
  0.0 89.1 jit_solution(2581889483758829855)
XLA Ops:
  0.0 0.0 copy-start
  0.0 2.2 %copy-done = bf16[2,8,1,256,2,1,256]{6,4,5,3,2,1,0:T(2,128)(2,1)S(1)} copy-done((bf16[2,8,1,256,2,1,256]{6,4,5,3,2,1,0:T(2,128)(2,1)S(1)}, bf16[2,8,1,256,2,1,256]{6,4,5,3,2,1,0:T(2,128)(2,1)}, u32[]{:S(2)}) %copy-start) | copy-done | bytes 4194328
  2.2 0.0 copy-start.2
  2.2 0.7 copy-done.2
  2.8 0.0 copy-start.1
  2.8 0.0 copy-start.3
  2.8 0.0 copy-start.4
  2.9 0.0 copy-start.5
  2.9 5.1 %split.1 = (bf16[2,4,4,256,256]{4,3,2,1,0:T(8,128)(2,1)S(1)}, bf16[16,2,128,256]{3,2,1,0:T(8,128)(2,1)S(1)}, bf16[16,2,128,256]{3,2,1,0:T(8,128)(2,1)S(1)}, bf16...) custom-call(s32[2]{0:T(128)S(1)} %copy-done.2, bf16[2,8,1024,128]{3,2,1,0:T(8,128)(2,1)S(1)} %bitcast.10), custom_call_target="tpu_custom_call" | custom-call | tf_op jit(solution)/shard_map/split/pallas_call | solution.py:415
  7.9 66.9 %gather_0.1 = (bf16[2,2,4,4,128,256]{5,4,3,2,1,0:T(8,128)(2,1)S(1)}, bf16[8,2,4,32,256]{4,3,2,1,0:T(8,128)(2,1)S(1)}, bf16[2,8,2,2,32,256]{5,4,3,2,1,0:T(8,128)(2,1)S(1)}) custom-call(s32[2]{0:T(128)S(1)} %copy-done.2, bf16[16,2,128,256]{3,2,1,0:T(8,128)(2,1)S(1)} %get-tuple-element.13.colq, bf16[16,2,128,256]{3,2,1,0:T(8,128)(2,1)S(1)} %get-tuple-element.14.col63, ...), custom_call_target="tpu_custom_call" | custom-call | tf_op jit(solution)/shard_map/gather_0/pallas_call | solution.py:352
  74.9 0.0 copy-done.1
  74.9 0.0 copy-done.3
  74.9 0.0 copy-done.4
  74.9 0.0 copy-done.5
  74.9 14.2 %update.1 = bf16[2,8,1024,128]{3,2,1,0:T(8,128)(2,1)} custom-call(s32[2]{0:T(128)S(1)} %copy-done.3, s32[2,64]{1,0:T(2,128)S(1)} %copy-done.4, s32[2,64]{1,0:T(2,128)S(1)} %copy-done.5, bf16[2,2,256,256]{3,2,1,0:T(8,128)(2,1)S(1)} %copy-done.1, bf16[2,2,4,4,128,256]{5,4,3,2,1,0:T(8,128)(2,1)S(1)} %get-tuple-element.17.x_ref, ...), custom_call_target="tpu_custom_call" | custom-call | tf_op jit(solution)/shard_map/update/pallas_call | solution.py:585
Async XLA Ops:
  0.0 2.2 %copy-start = (bf16[2,8,1,256,2,1,256]{6,4,5,3,2,1,0:T(2,128)(2,1)S(1)}, bf16[2,8,1,256,2,1,256]{6,4,5,3,2,1,0:T(2,128)(2,1)}, u32[]{:S(2)}) copy-start(bf16[2,8,1,256,2,1,256]{6,4,5,3,2,1,0:T(2,128)(2,1)} %param.5) | copy-start | bytes 12582916
  2.2 0.7 copy-start.2
  2.8 72.0 %copy-start.1 = (bf16[2,2,256,256]{3,2,1,0:T(8,128)(2,1)S(1)}, bf16[2,2,256,256]{3,2,1,0:T(8,128)(2,1)}, u32[]{:S(2)}) copy-start(bf16[2,2,256,256]{3,2,1,0:T(8,128)(2,1)} %inv_ref.1) | copy-start | bytes 1572868
  2.8 72.0 %copy-start.3 = (s32[2]{0:T(128)S(1)}, s32[2]{0:T(128)}, u32[]{:S(2)}) copy-start(s32[2]{0:T(128)} %piv_ref.5) | copy-start | bytes 28
  2.8 72.0 %copy-start.4 = (s32[2,64]{1,0:T(2,128)S(1)}, s32[2,64]{1,0:T(2,128)}, u32[]{:S(2)}) copy-start(s32[2,64]{1,0:T(2,128)} %cl_ref.1) | copy-start | bytes 1540
  2.9 72.0 %copy-start.5 = (s32[2,64]{1,0:T(2,128)S(1)}, s32[2,64]{1,0:T(2,128)}, u32[]{:S(2)}) copy-start(s32[2,64]{1,0:T(2,128)} %rl_ref.1) | copy-start | bytes 1540

commit v3 on v2

--- a/solution.py
+++ b/solution.py
@@ -13,9 +13,9 @@
 
 def gather_kernel(
     piv_ref, colq, col63, rowq, row63, xbuf, ubuf, kbuf,
-    other_q, picked, from_chips, other_63, xown, from_rows, uown, mine_c, other_c, from_x, picked_c, from_y, kown,
-    s_half, s_col, s_col63, s_ax, s_ay, s_row, s_row63, s_urow, s_cor, s_cx, s_cy, s_krow, s_xsib, s_ksib,
-    r_half, r_col, r_col63, r_ax, r_ay, r_row, r_row63, r_urow, r_cor, r_cx, r_cy, r_krow, r_xsib, r_ksib,
+    other_q, picked, from_1, relay_1, got_1, from_2, relay_2, other_63, xown, from_rows, uown, mine_c, other_c, from_x, picked_c, from_y, kown, relay,
+    s_half, s_e1, s_e2, s_col63, s_ax, s_ay, s_row, s_row63, s_urow, s_cor, s_cx, s_cy, s_krow, s_xsib, s_ksib, s_relay,
+    r_half, r_e1, r_e2, r_col63, r_ax, r_ay, r_row, r_row63, r_urow, r_cor, r_cx, r_cy, r_krow, r_xsib, r_ksib, r_relay,
 ):
     z = lax.axis_index("row")
     c = lax.axis_index("col")
@@ -94,41 +94,96 @@
     def _():
         half_63.wait_recv()
 
+    def part_63(p, dst, sem, i, rsem, to):
+        @pl.when(core == 0)
+        def _():
+            remote(other_63.at[p], dst, sem.at[i], rsem, to).start()
+
+        @pl.when(core == 1)
+        def _():
+            remote(col63.at[p, 1], dst, sem.at[i], rsem, to).start()
+
     @pl.when(last_chip)
     def _():
         def send_63(i, carry):
             p = to_chip(i)
-
-            @pl.when(core == 0)
+            relayed = (p % 4 == 1) & (p // 4 != 3)
+
+            @pl.when(jnp.logical_not(relayed))
             def _():
-                remote(other_63.at[p], xown.at[1], s_col63.at[i], r_col63.at[0], on_chip(p)).start()
-
-            @pl.when(core == 1)
+                part_63(p, xown.at[1], s_col63, i, r_col63.at[0], on_chip(p))
+
+            @pl.when(relayed)
             def _():
-                remote(col63.at[p, 1], xown.at[1], s_col63.at[i], r_col63.at[0], on_chip(p)).start()
+                part_63(p, relay, s_col63, i, r_relay.at[0], on_chip(p + 2))
             return carry
 
         lax.fori_loop(1, 16, send_63, 0)
 
     half_q.wait_recv()
 
+    first_x = core == 0
+    a1, a2 = jnp.where(first_x, cx, cy), jnp.where(first_x, cy, cx)
+    q1, q2 = jnp.where(first_x, q_chip % 4, q_chip // 4), jnp.where(first_x, q_chip // 4, q_chip % 4)
+
+    def axis1(v):
+        return on_chip(jnp.where(first_x, cy * 4 + v, v * 4 + cx))
+
+    def axis2(v):
+        return on_chip(jnp.where(first_x, v * 4 + cx, cy * 4 + v))
+
     def pick(i, carry):
-        picked[i] = jnp.where(q_here, colq[i, core], other_q[i])
+        v, w = i // 4, i % 4
+        p = jnp.where(first_x, w * 4 + v, v * 4 + w)
+        picked[v, w] = jnp.where(q_here, colq[p, core], other_q[p])
         return carry
 
     lax.fori_loop(0, 16, pick, 0)
 
-    def send_col(i, carry):
-        p = to_chip(i)
-        remote(picked.at[p], from_chips.at[chip], s_col.at[i], r_col.at[chip], on_chip(p)).start()
-        return carry
-
-    lax.fori_loop(1, 16, send_col, 0)
-    from_chips[chip] = picked[chip]
+    def exchange_start(parts, got, relays, half, ssem, rsem, me, on):
+        up, down, far = lax.rem(me + 1, 4), lax.rem(me + 3, 4), lax.rem(me + 2, 4)
+        remote(parts.at[up], got.at[me], ssem.at[0], rsem.at[0], on(up)).start()
+        remote(parts.at[down], got.at[me], ssem.at[1], rsem.at[1], on(down)).start()
+        remote(parts.at[far, half(0)], relays.at[0], ssem.at[2], rsem.at[2], on(up)).start()
+        remote(parts.at[far, half(1)], relays.at[1], ssem.at[3], rsem.at[3], on(down)).start()
+        got[me] = parts[me]
+
+    def exchange_pass(parts, got, relays, half, ssem, rsem, me, on):
+        up, down = lax.rem(me + 1, 4), lax.rem(me + 3, 4)
+        remote(relays.at[0], relays.at[0], ssem.at[2], rsem.at[2], on(down)).wait_recv()
+        remote(relays.at[0], got.at[down, half(0)], ssem.at[4], rsem.at[4], on(up)).start()
+        remote(relays.at[1], relays.at[1], ssem.at[3], rsem.at[3], on(up)).wait_recv()
+        remote(relays.at[1], got.at[up, half(1)], ssem.at[5], rsem.at[5], on(down)).start()
+
+    def exchange_end(parts, got, relays, half, ssem, rsem, me, on):
+        up, down, far = lax.rem(me + 1, 4), lax.rem(me + 3, 4), lax.rem(me + 2, 4)
+        remote(got.at[down], got.at[down], ssem.at[0], rsem.at[0], on(down)).wait_recv()
+        remote(got.at[up], got.at[up], ssem.at[1], rsem.at[1], on(up)).wait_recv()
+        remote(relays.at[0], got.at[far, half(0)], ssem.at[4], rsem.at[4], on(down)).wait_recv()
+        remote(relays.at[1], got.at[far, half(1)], ssem.at[5], rsem.at[5], on(up)).wait_recv()
+
+    def exchange_sent(parts, got, relays, half, ssem, rsem, me, on):
+        for i in range(6):
+            part = parts.at[0] if i < 2 else relays.at[0]
+            remote(part, part, ssem.at[i], rsem.at[i], on(me)).wait_send()
+
+    stage1 = (picked, from_1, relay_1, lambda h: pl.ds(2 * h, 2), s_e1, r_e1, a1, axis1)
+    stage2 = (got_1, from_2, relay_2, lambda h: pl.ds(h * (HALF // 2), HALF // 2), s_e2, r_e2, a2, axis2)
+
+    exchange_start(*stage1)
+    relays = (cx == 3) & jnp.logical_not(last_chip)
+    pass_63 = remote(relay, xown.at[1], s_relay.at[0], r_col63.at[0], on_chip(jnp.where(relays, chip - 2, chip)))
+
+    @pl.when(relays)
+    def _():
+        remote(relay, relay, s_relay.at[0], r_relay.at[0], on_chip(chip)).wait_recv()
+        pass_63.start()
 
     @pl.when(last_chip)
     def _():
         xown[1] = jnp.where(core == 0, other_63[15], col63[15, 1])
+
+    exchange_pass(*stage1)
 
     from_rows[z] = rowq[z]
 
@@ -227,6 +282,9 @@
     ring_u = (lambda w: ubuf.at[w], s_urow, r_urow)
     ring_k = (lambda w: kbuf.at[core, w], s_krow, r_krow)
 
+    def to_sibling(part, i):
+        remote(part, part, s_xsib.at[i], r_xsib.at[i], sibling).start()
+
     cor.wait_recv()
     for b, here in ((0, q_here), (1, core == 1)):
         from_x[cx, b] = jnp.where(here, mine_c[core, b], other_c[b])
@@ -234,6 +292,9 @@
         remote(from_x.at[cx], from_x.at[cx], s_cx.at[i], r_cx.at[cx], on_x(x_mate(i))).start()
     ring_send(ring_u, uown)
     ubuf[z] = uown[...]
+    exchange_end(*stage1)
+    got_1[...] = from_1[q1]
+    exchange_start(*stage2)
     for i in range(1, 4):
         v = x_mate(i)
         remote(from_x.at[v], from_x.at[v], s_cx.at[i], r_cx.at[v], on_x(v)).wait_recv()
@@ -242,6 +303,7 @@
     for i in range(1, 4):
         remote(picked_c, from_y.at[cy], s_cy.at[i], r_cy.at[cy], on_y(y_mate(i))).start()
     from_y[cy] = picked_c[...]
+    exchange_pass(*stage2)
     ring_pass(ring_u, 1)
 
     for i in range(1, 4):
@@ -260,32 +322,64 @@
     xbuf[1, core, cy, cx] = xown[1]
     ring_pass(ring_u, 2)
 
-    def wait_col(i, carry):
-        p = to_chip(i)
-        remote(from_chips.at[p], from_chips.at[p], s_col.at[i], r_col.at[p], on_chip(p)).wait_recv()
-        return carry
-
-    lax.fori_loop(1, 16, wait_col, 0)
-    xown[0] = from_chips[q_chip]
+    exchange_end(*stage2)
+    xown[0] = from_2[q2]
     line_send(line_qx, xown.at[0])
     xbuf[0, core, cy, cx] = xown[0]
     ring_pass(ring_k, 1)
     line_pass(line_63y)
     line_pass(line_qx)
+    ring_pass(ring_k, 2)
     ring_pass(ring_u, 3)
-    ring_pass(ring_k, 2)
     line_end(line_63y)
     line_send(line_63x, x_lines(cx))
+    to_sibling(x_lines(cx), 4)
     line_end(line_qx)
     line_send(line_qy, y_lines(cy))
 
-    def to_sibling(part, i):
-        remote(part, part, s_xsib.at[i], r_xsib.at[i], sibling).start()
-
     to_sibling(xbuf.at[0, core, cy], 0)
+
+    half_q.wait_send()
+    cor.wait_send()
+
+    @pl.when(last_chip & (core == 1))
+    def _():
+        half_63.wait_send()
+
+    @pl.when(relays)
+    def _():
+        pass_63.wait_send()
+
+    def sent_rows(i, carry):
+        to = on_row(to_row(i))
+        remote(rowq.at[0], from_rows.at[0], s_row.at[i], r_row.at[0], to).wait_send()
+
+        @pl.when(z == 7)
+        def _():
+            remote(row63.at[0], uown.at[1], s_row63.at[i], r_row63.at[0], to).wait_send()
+        return carry
+
+    lax.fori_loop(1, 8, sent_rows, 0)
+
+    @pl.when(last_chip)
+    def _():
+        def sent_chips(i, carry):
+            remote(xown.at[1], xown.at[1], s_col63.at[i], r_col63.at[0], sibling).wait_send()
+            return carry
+
+        lax.fori_loop(1, 16, sent_chips, 0)
+
+    exchange_sent(*stage1)
+    exchange_sent(*stage2)
+    line_sent(line_63y, xown.at[1])
+    line_sent(line_qx, xown.at[0])
+    for i in range(1, 4):
+        remote(picked_c, picked_c, s_cx.at[i], r_cx.at[0], sibling).wait_send()
+        remote(picked_c, picked_c, s_cy.at[i], r_cy.at[0], sibling).wait_send()
     ring_pass(ring_k, 3)
-    ring_pass(ring_u, 4)
     line_pass(line_63x)
+    to_sibling(x_lines(x_mate(1)), 5)
+    to_sibling(x_lines(x_mate(3)), 7)
     line_pass(line_qy)
     ring_pass(ring_k, 4)
     both = remote(kbuf.at[core], kbuf.at[core], s_ksib.at[0], r_ksib.at[0], sibling)
@@ -293,52 +387,20 @@
     to_sibling(xbuf.at[0, core, y_mate(1)], 1)
     to_sibling(xbuf.at[0, core, y_mate(3)], 3)
     line_end(line_63x)
-    to_sibling(xbuf.at[1, core], 4)
+    to_sibling(x_lines(x_mate(2)), 6)
+    ring_pass(ring_u, 4)
+    ring_sent(ring_u)
     line_end(line_qy)
     to_sibling(xbuf.at[0, core, y_mate(2)], 2)
 
-    half_q.wait_send()
-    cor.wait_send()
-
-    @pl.when(last_chip & (core == 1))
-    def _():
-        half_63.wait_send()
-
-    def sent_rows(i, carry):
-        to = on_row(to_row(i))
-        remote(rowq.at[0], from_rows.at[0], s_row.at[i], r_row.at[0], to).wait_send()
-
-        @pl.when(z == 7)
-        def _():
-            remote(row63.at[0], uown.at[1], s_row63.at[i], r_row63.at[0], to).wait_send()
-        return carry
-
-    lax.fori_loop(1, 8, sent_rows, 0)
-
-    def sent_chips(i, carry):
-        to = on_chip(to_chip(i))
-        remote(picked.at[0], from_chips.at[0], s_col.at[i], r_col.at[0], to).wait_send()
-
-        @pl.when(last_chip)
-        def _():
-            remote(picked.at[0], xown.at[1], s_col63.at[i], r_col63.at[0], to).wait_send()
-        return carry
-
-    lax.fori_loop(1, 16, sent_chips, 0)
-    ring_sent(ring_u)
     ring_sent(ring_k)
-    line_sent(line_63y, xown.at[1])
     line_sent(line_63x, x_lines(cx))
-    line_sent(line_qx, xown.at[0])
     line_sent(line_qy, y_lines(cy))
-    for i in range(1, 4):
-        remote(picked_c, picked_c, s_cx.at[i], r_cx.at[0], sibling).wait_send()
-        remote(picked_c, picked_c, s_cy.at[i], r_cy.at[0], sibling).wait_send()
     for i in range(4):
         line = xbuf.at[0, 1 - core, y_mate(i)]
         remote(line, line, s_xsib.at[i], r_xsib.at[i], sibling).wait()
-    whole = xbuf.at[1, 1 - core]
-    remote(whole, whole, s_xsib.at[4], r_xsib.at[4], sibling).wait()
+        line = xbuf.at[1, 1 - core, :, x_mate(i)]
+        remote(line, line, s_xsib.at[4 + i], r_xsib.at[4 + i], sibling).wait()
     both.wait_send()
     remote(kbuf.at[1 - core], kbuf.at[1 - core], s_ksib.at[0], r_ksib.at[0], sibling).wait_recv()
 
@@ -348,7 +410,7 @@
     shape = jax.ShapeDtypeStruct
     vmem = pl.BlockSpec(memory_space=pltpu.VMEM)
     dma = pltpu.SemaphoreType.DMA
-    sems = [dma(n) for n in ((2,), (16,), (16,), (2, 6), (2, 6), (8,), (8,), (8,), (1,), (4,), (4,), (8,), (5,), (1,))]
+    sems = [dma(n) for n in ((2,), (6,), (6,), (16,), (2, 6), (2, 6), (8,), (8,), (8,), (1,), (4,), (4,), (8,), (8,), (1,), (1,))]
     return pl.pallas_call(
         gather_kernel,
         name="gather_0",
@@ -360,12 +422,13 @@
         in_specs=[pl.BlockSpec(memory_space=pltpu.SMEM)] + [vmem] * 4,
         out_specs=[vmem] * 3,
         scratch_shapes=[
-            pltpu.VMEM((16, HALF, B), bf), pltpu.VMEM((16, HALF, B), bf), pltpu.VMEM((16, HALF, B), bf),
-            pltpu.VMEM((16, HALF, B), bf), pltpu.VMEM((2, HALF, B), bf),
+            pltpu.VMEM((16, HALF, B), bf), pltpu.VMEM((4, 4, HALF, B), bf), pltpu.VMEM((4, 4, HALF, B), bf),
+            pltpu.VMEM((2, 2, HALF, B), bf), pltpu.VMEM((4, HALF, B), bf), pltpu.VMEM((4, HALF, B), bf),
+            pltpu.VMEM((2, HALF // 2, B), bf), pltpu.VMEM((16, HALF, B), bf), pltpu.VMEM((2, HALF, B), bf),
             pltpu.VMEM((8, 4, SLAB, B), bf), pltpu.VMEM((2, 4, SLAB, B), bf),
             pltpu.VMEM((2, 2, 2, SLAB, B), bf), pltpu.VMEM((2, 2, SLAB, B), bf),
             pltpu.VMEM((4, 2, 2, SLAB, B), bf), pltpu.VMEM((2, 2, SLAB, B), bf),
-            pltpu.VMEM((4, 2, 2, SLAB, B), bf), pltpu.VMEM((2, 2, SLAB, B), bf),
+            pltpu.VMEM((4, 2, 2, SLAB, B), bf), pltpu.VMEM((2, 2, SLAB, B), bf), pltpu.VMEM((HALF, B), bf),
         ] + sems + sems,
         compiler_params=pltpu.CompilerParams(collective_id=0, has_side_effects=True, vmem_limit_bytes=24 * 2**20),
     )(pivots, colq, col63, rowq, row63)
@@ -480,20 +543,55 @@
 
     @pl.when(group == 0)
     def _():
-        def refine(diagonal, step, keep, keep_right):
+        def refine(diagonal, step, keep, keep_right, *meanwhile):
             guess = (inv_ref[step, 0], inv_ref[step, 1])
             store_right(tmp, guess)
             eye = lax.broadcasted_iota(jnp.int32, (B, B), 0) == lax.broadcasted_iota(jnp.int32, (B, B), 1)
             real, imag = halves(dot(diagonal, tmp[...]))
+            if meanwhile:
+                meanwhile[0]()
             store_right(tmp, ((jnp.where(eye, 2.0, 0.0) - real).astype(bf), (-imag).astype(bf)))
             keep[...] = dot(flat(guess), tmp[...]).astype(bf)
+            if meanwhile:
+                meanwhile[1]()
             store_right(keep_right, halves(keep[...]))
 
+        def panel(s, q):
+            return jnp.concatenate(
+                [flat([from_column(s, r, 2 * q + t) for r in range(2)]) for t in range(2)], axis=0
+            )
+
+        def mixed(q, product, old, which):
+            return jnp.concatenate(
+                [
+                    jnp.where(taken((2 * q + t) * 8 + z)[which], product[t * B:(t + 1) * B], old[t * B:(t + 1) * B])
+                    for t in range(2)
+                ],
+                axis=0,
+            ).astype(bf)
+
+        def both(q):
+            return pl.ds(2 * q * B, 2 * B)
+
+        def first_panel(q):
+            old = panel(s0, q)
+            l0[both(q), :] = mixed(q, dot(old, rx0[...]), old.astype(f32), 0)
+
+        def moved_panel(q):
+            old = panel(s1, q).astype(f32)
+            l1[both(q), :] = mixed(q, old - dot(l0[both(q), :], rm01[...]), old, 0)
+
+        def second_panel(q):
+            moved = l1[both(q), :]
+            l1[both(q), :] = mixed(q, dot(moved, rx1[...]), moved.astype(f32), 1)
+
+        store_right(rm01, corner(s0, s1))
         refine(flat(corner(s0, s0)), 0, f0, rx0)
         l10 = dot(flat(corner(s1, s0)), rx0[...]).astype(bf)
-        store_right(rm01, corner(s0, s1))
+        first_panel(0)
         m11 = (flat(corner(s1, s1)).astype(f32) - dot(l10, rm01[...])).astype(bf)
-        refine(m11, 1, f1, rx1)
+        first_panel(1)
+        refine(m11, 1, f1, rx1, lambda: (first_panel(2), first_panel(3)), lambda: (moved_panel(0), moved_panel(1)))
         for tc in range(2):
             store_right(ru0, (from_row(s0, 2 * tc), from_row(s0, 2 * tc + 1)), tc * B, 2 * B)
         product = dot(l10, ru0[...])
@@ -504,29 +602,11 @@
                 at = (2 * r + tc) * B
                 pair.append(jnp.where(cols0[tc], old - product[:, at:at + B], old).astype(bf))
             store_right(ru1, pair, tc * B, 2 * B)
+
+        moved_panel(2)
+        moved_panel(3)
         for q in range(4):
-            flags = [taken((2 * q + t) * 8 + z) for t in range(2)]
-            rows = [pl.ds((2 * q + t) * B, B) for t in range(2)]
-            both = pl.ds(2 * q * B, 2 * B)
-
-            def panel(s, q=q):
-                return jnp.concatenate([flat([from_column(s, r, 2 * q + t) for r in range(2)]) for t in range(2)], axis=0)
-
-            def mixed(product, old, which):
-                return jnp.concatenate(
-                    [
-                        jnp.where(flags[t][which], product[t * B:(t + 1) * B], old[t * B:(t + 1) * B])
-                        for t in range(2)
-                    ],
-                    axis=0,
-                ).astype(bf)
-
-            old = panel(s0)
-            left = mixed(dot(old, rx0[...]), old.astype(f32), 0)
-            l0[both, :] = left
-            old = panel(s1).astype(f32)
-            moved = mixed(old - dot(left, rm01[...]), old, 0)
-            l1[both, :] = mixed(dot(moved, rx1[...]), moved.astype(f32), 1)
+            second_panel(q)
 
     first = dot(l0[pl.ds(2 * group * B, 2 * B), :], ru0[...])
     second = dot(l1[pl.ds(2 * group * B, 2 * B), :], ru1[...])

time: 89.2 us -> 86.9 us (0.974)
  Pallas kernels: 86.2 us -> 83.9 us
    pallas_call x1, Pallas kernels: 66.9 us -> 64.9 us  [gather(): pl.pallas_call(gather_kernel, name='gather_0', out_shape=[shape((2, 2, 4,...]
where the time goes in v3:
time: 86.9 us; the launch traced here: 86.8 us
  Pallas kernels  83.9 us (97%)
  local copies, waits for them, and re-layouts  2.86 us (3%)
    pallas_call x1, Pallas kernels, gather(): pl.pallas_call(gather_kernel, name='gather_0', out_shape=[shape((2, 2, 4,...  64.9 us
    pallas_call x1, Pallas kernels, update(): pl.pallas_call(update_kernel, name='update', grid=(4,), out_shape=jax.Sha...  13.9 us
    pallas_call x1, Pallas kernels, split(): pl.pallas_call(split_kernel, name='split', grid=(4,), out_shape=[shape((2...  5.07 us
    unnamed x12, local copies, waits for them, and re-layouts  2.86 us

profile of v3, /device:TPU:1, one launch (start us, length us, event | category | flops | bytes accessed | tf_op | source)
XLA Modules:
  0.0 86.8 jit_solution(14885528699546648159)
XLA Ops:
  0.0 0.0 copy-start
  0.0 2.2 %copy-done = bf16[2,8,1,256,2,1,256]{6,4,5,3,2,1,0:T(2,128)(2,1)S(1)} copy-done((bf16[2,8,1,256,2,1,256]{6,4,5,3,2,1,0:T(2,128)(2,1)S(1)}, bf16[2,8,1,256,2,1,256]{6,4,5,3,2,1,0:T(2,128)(2,1)}, u32[]{:S(2)}) %copy-start) | copy-done | bytes 4194328
  2.2 0.0 copy-start.2
  2.2 0.7 copy-done.2
  2.8 0.0 copy-start.1
  2.8 0.0 copy-start.3
  2.8 0.0 copy-start.4
  2.9 0.0 copy-start.5
  2.9 5.1 %split.1 = (bf16[2,4,4,256,256]{4,3,2,1,0:T(8,128)(2,1)S(1)}, bf16[16,2,128,256]{3,2,1,0:T(8,128)(2,1)S(1)}, bf16[16,2,128,256]{3,2,1,0:T(8,128)(2,1)S(1)}, bf16...) custom-call(s32[2]{0:T(128)S(1)} %copy-done.2, bf16[2,8,1024,128]{3,2,1,0:T(8,128)(2,1)S(1)} %bitcast.10), custom_call_target="tpu_custom_call" | custom-call | tf_op jit(solution)/shard_map/split/pallas_call | solution.py:478
  7.9 64.9 %gather_0.1 = (bf16[2,2,4,4,128,256]{5,4,3,2,1,0:T(8,128)(2,1)S(1)}, bf16[8,2,4,32,256]{4,3,2,1,0:T(8,128)(2,1)S(1)}, bf16[2,8,2,2,32,256]{5,4,3,2,1,0:T(8,128)(2,1)S(1)}) custom-call(s32[2]{0:T(128)S(1)} %copy-done.2, bf16[16,2,128,256]{3,2,1,0:T(8,128)(2,1)S(1)} %get-tuple-element.13.colq, bf16[16,2,128,256]{3,2,1,0:T(8,128)(2,1)S(1)} %get-tuple-element.14.col63, ...), custom_call_target="tpu_custom_call" | custom-call | tf_op jit(solution)/shard_map/gather_0/pallas_call | solution.py:414
  72.8 0.0 copy-done.1
  72.8 0.0 copy-done.3
  72.8 0.0 copy-done.4
  72.9 0.0 copy-done.5
  72.9 13.9 %update.1 = bf16[2,8,1024,128]{3,2,1,0:T(8,128)(2,1)} custom-call(s32[2]{0:T(128)S(1)} %copy-done.3, s32[2,64]{1,0:T(2,128)S(1)} %copy-done.4, s32[2,64]{1,0:T(2,128)S(1)} %copy-done.5, bf16[2,2,256,256]{3,2,1,0:T(8,128)(2,1)S(1)} %copy-done.1, bf16[2,2,4,4,128,256]{5,4,3,2,1,0:T(8,128)(2,1)S(1)} %get-tuple-element.17.x_ref, ...), custom_call_target="tpu_custom_call" | custom-call | tf_op jit(solution)/shard_map/update/pallas_call | solution.py:665
Async XLA Ops:
  0.0 2.2 %copy-start = (bf16[2,8,1,256,2,1,256]{6,4,5,3,2,1,0:T(2,128)(2,1)S(1)}, bf16[2,8,1,256,2,1,256]{6,4,5,3,2,1,0:T(2,128)(2,1)}, u32[]{:S(2)}) copy-start(bf16[2,8,1,256,2,1,256]{6,4,5,3,2,1,0:T(2,128)(2,1)} %param.5) | copy-start | bytes 12582916
  2.2 0.7 copy-start.2
  2.8 70.0 %copy-start.1 = (bf16[2,2,256,256]{3,2,1,0:T(8,128)(2,1)S(1)}, bf16[2,2,256,256]{3,2,1,0:T(8,128)(2,1)}, u32[]{:S(2)}) copy-start(bf16[2,2,256,256]{3,2,1,0:T(8,128)(2,1)} %inv_ref.1) | copy-start | bytes 1572868
  2.8 70.0 %copy-start.3 = (s32[2]{0:T(128)S(1)}, s32[2]{0:T(128)}, u32[]{:S(2)}) copy-start(s32[2]{0:T(128)} %piv_ref.5) | copy-start | bytes 28
  2.8 70.0 %copy-start.4 = (s32[2,64]{1,0:T(2,128)S(1)}, s32[2,64]{1,0:T(2,128)}, u32[]{:S(2)}) copy-start(s32[2,64]{1,0:T(2,128)} %cl_ref.1) | copy-start | bytes 1540
  2.9 70.0 %copy-start.5 = (s32[2,64]{1,0:T(2,128)S(1)}, s32[2,64]{1,0:T(2,128)}, u32[]{:S(2)}) copy-start(s32[2,64]{1,0:T(2,128)} %rl_ref.1) | copy-start | bytes 1540

commit v4 on v3

--- a/solution.py
+++ b/solution.py
@@ -443,20 +443,18 @@
     for r in range(2):
         for t in range(2):
             j = 2 * r + t
-            for half in range(2):
-                pair = jnp.concatenate([m_ref[r, t, pl.ds((2 * half + s) * B, B), :] for s in range(2)], axis=1)
-                sorted_rows = jnp.dot(perm, pair, preferred_element_type=jnp.float32).astype(jnp.bfloat16)
-                for s in range(2):
-                    for lb in range(2):
-                        for tc in range(2):
-                            piece = sorted_rows[(lb * 2 + tc) * 64:(lb * 2 + tc + 1) * 64, s * 128:(s + 1) * 128]
-                            here = (pl.ds((2 * half + s) * 64, 64), pl.ds(lb * 128, 128))
-                            d_ref[(tc, group, j, *here)] = piece
-
+            parts = jnp.concatenate([m_ref[r, t, pl.ds(s * B, B), :] for s in range(4)], axis=1)
+            sorted_rows = jnp.dot(perm, parts, preferred_element_type=jnp.float32).astype(jnp.bfloat16)
+            for s in range(4):
+                for lb in range(2):
+                    for tc in range(2):
+                        piece = sorted_rows[(lb * 2 + tc) * 64:(lb * 2 + tc + 1) * 64, s * 128:(s + 1) * 128]
+                        lanes = pl.ds(lb * 128, 128)
+                        d_ref[tc, group, j, pl.ds(s * 64, 64), lanes] = piece
+                        if tc == 1:
+                            col63_ref[8 * r + 2 * group + t, s // 2, pl.ds(s % 2 * 64, 64), lanes] = piece
             for h in range(2):
-                rows = pl.ds(h * HALF, HALF)
-                colq_ref[8 * r + 2 * group + t, h] = d_ref[other // 32, group, j, rows]
-                col63_ref[8 * r + 2 * group + t, h] = d_ref[1, group, j, rows]
+                colq_ref[8 * r + 2 * group + t, h] = d_ref[other // 32, group, j, pl.ds(h * HALF, HALF)]
 
             @pl.when(other // 8 == 2 * group + t)
             def _(r=r, j=j):
@@ -608,15 +606,15 @@
         for q in range(4):
             second_panel(q)
 
-    first = dot(l0[pl.ds(2 * group * B, 2 * B), :], ru0[...])
-    second = dot(l1[pl.ds(2 * group * B, 2 * B), :], ru1[...])
-    for t in range(2):
-        take0, take1 = taken((2 * group + t) * 8 + z)
+    first = dot(l0[pl.ds(4 * group * B, 4 * B), :], ru0[...])
+    second = dot(l1[pl.ds(4 * group * B, 4 * B), :], ru1[...])
+    for t in range(4):
+        take0, take1 = taken((4 * group + t) * 8 + z)
         for tc in range(2):
             use0 = take0 & cols0[tc] & (col_ids[tc] != p1)
             use1 = take1 & cols1[tc]
             for r in range(2):
-                old = d_ref[tc, group, 2 * r + t].astype(f32)
+                old = d_ref[tc, 2 * group + t // 2, 2 * r + t % 2].astype(f32)
                 at = (2 * r + tc) * B
                 rows = slice(t * B, (t + 1) * B)
                 old = jnp.where(use0, old - first[rows, at:at + B], old).astype(bf).astype(f32)
@@ -626,33 +624,31 @@
         for pivot, left, factor in ((p0, l0, f0), (p1, l1, f1)):
             @pl.when(col_ids[tc] == pivot)
             def _(tc=tc, pivot=pivot, left=left, factor=factor):
-                for t in range(2):
-                    is_pivot = (2 * group + t) * 8 + z == pivot
+                for t in range(4):
+                    is_pivot = (4 * group + t) * 8 + z == pivot
                     for r in range(2):
                         lanes = pl.ds(r * B, B)
-                        other = left[pl.ds((2 * group + t) * B, B), lanes].astype(f32)
+                        other = left[pl.ds((4 * group + t) * B, B), lanes].astype(f32)
                         tile[t, tc, r] = jnp.where(is_pivot, factor[:, lanes].astype(f32), other).astype(bf)
 
     out_row = lax.broadcasted_iota(jnp.int32, (B, B), 0)
     in_row = lax.broadcasted_iota(jnp.int32, (B, B), 1)
     perm = jnp.where(out_row == (in_row % 64) * 4 + in_row // 64, 1.0, 0.0).astype(bf)
-    for t in range(2):
+    for t in range(4):
         for r in range(2):
-            for half in range(2):
-                stacked = jnp.concatenate(
-                    [
-                        jnp.concatenate(
-                            [tile[t, tc, r, pl.ds((2 * half + s) * 64, 64), pl.ds(lb * 128, 128)] for s in range(2)],
-                            axis=1,
-                        )
-                        for lb in range(2)
-                        for tc in range(2)
-                    ],
-                    axis=0,
-                )
-                woven = dot(perm, stacked).astype(bf)
-                for s in range(2):
-                    o_ref[r, t, pl.ds((2 * half + s) * B, B), :] = woven[:, s * 128:(s + 1) * 128]
+            stacked = jnp.concatenate(
+                [
+                    jnp.concatenate(
+                        [tile[t, tc, r, pl.ds(s * 64, 64), pl.ds(lb * 128, 128)] for s in range(4)], axis=1
+                    )
+                    for lb in range(2)
+                    for tc in range(2)
+                ],
+                axis=0,
+            )
+            woven = dot(perm, stacked).astype(bf)
+            for s in range(4):
+                o_ref[r, t, pl.ds(s * B, B), :] = woven[:, s * 128:(s + 1) * 128]
 
 
 def update(pivots, col_lists, row_lists, inverses, x, u, k, d):
@@ -665,13 +661,13 @@
     return pl.pallas_call(
         update_kernel,
         name="update",
-        grid=(4,),
+        grid=(2,),
         out_shape=jax.ShapeDtypeStruct((2, 8, 4 * B, 128), jnp.bfloat16),
         in_specs=[smem] * 3 + [vmem_in] * 5,
-        out_specs=pl.BlockSpec((2, 2, 4 * B, 128), lambda g: (0, g, 0, 0)),
+        out_specs=pl.BlockSpec((2, 4, 4 * B, 128), lambda g: (0, g, 0, 0)),
         scratch_shapes=[
             flat_square, flat_square, square, square, square, wide, wide, square, panel, panel,
-            pltpu.VMEM((2, 2, 2, B, B), jnp.bfloat16),
+            pltpu.VMEM((4, 2, 2, B, B), jnp.bfloat16),
         ],
         compiler_params=pltpu.CompilerParams(vmem_limit_bytes=32 * 2**20),
     )(pivots, col_lists, row_lists, inverses, x, u, k, d)

time: 86.9 us -> 86.2 us (level)
  no operation moved by 1% of the time
where the time goes in v4:
time: 86.2 us; the launch traced here: 86.1 us
  Pallas kernels  83.2 us (97%)
  local copies, waits for them, and re-layouts  2.86 us (3%)
    pallas_call x1, Pallas kernels, gather(): pl.pallas_call(gather_kernel, name='gather_0', out_shape=[shape((2, 2, 4,...  64.7 us
    pallas_call x1, Pallas kernels, update(): pl.pallas_call(update_kernel, name='update', grid=(2,), out_shape=jax.Sha...  13.7 us
    pallas_call x1, Pallas kernels, split(): pl.pallas_call(split_kernel, name='split', grid=(4,), out_shape=[shape((2...  4.83 us
    unnamed x12, local copies, waits for them, and re-layouts  2.86 us

profile of v4, /device:TPU:1, one launch (start us, length us, event | category | flops | bytes accessed | tf_op | source)
XLA Modules:
  0.0 86.1 jit_solution(6497942763365904586)
XLA Ops:
  0.0 0.0 copy-start
  0.0 2.2 %copy-done = bf16[2,8,1,256,2,1,256]{6,4,5,3,2,1,0:T(2,128)(2,1)S(1)} copy-done((bf16[2,8,1,256,2,1,256]{6,4,5,3,2,1,0:T(2,128)(2,1)S(1)}, bf16[2,8,1,256,2,1,256]{6,4,5,3,2,1,0:T(2,128)(2,1)}, u32[]{:S(2)}) %copy-start) | copy-done | bytes 4194328
  2.2 0.0 copy-start.2
  2.2 0.7 copy-done.2
  2.8 0.0 copy-start.1
  2.8 0.0 copy-start.3
  2.8 0.0 copy-start.4
  2.9 0.0 copy-start.5
  2.9 4.8 %split.1 = (bf16[2,4,4,256,256]{4,3,2,1,0:T(8,128)(2,1)S(1)}, bf16[16,2,128,256]{3,2,1,0:T(8,128)(2,1)S(1)}, bf16[16,2,128,256]{3,2,1,0:T(8,128)(2,1)S(1)}, bf16...) custom-call(s32[2]{0:T(128)S(1)} %copy-done.2, bf16[2,8,1024,128]{3,2,1,0:T(8,128)(2,1)S(1)} %bitcast.10), custom_call_target="tpu_custom_call" | custom-call | tf_op jit(solution)/shard_map/split/pallas_call | solution.py:476
  7.7 64.7 %gather_0.1 = (bf16[2,2,4,4,128,256]{5,4,3,2,1,0:T(8,128)(2,1)S(1)}, bf16[8,2,4,32,256]{4,3,2,1,0:T(8,128)(2,1)S(1)}, bf16[2,8,2,2,32,256]{5,4,3,2,1,0:T(8,128)(2,1)S(1)}) custom-call(s32[2]{0:T(128)S(1)} %copy-done.2, bf16[16,2,128,256]{3,2,1,0:T(8,128)(2,1)S(1)} %get-tuple-element.13.colq, bf16[16,2,128,256]{3,2,1,0:T(8,128)(2,1)S(1)} %get-tuple-element.14.col63, ...), custom_call_target="tpu_custom_call" | custom-call | tf_op jit(solution)/shard_map/gather_0/pallas_call | solution.py:414
  72.4 0.0 copy-done.1
  72.4 0.0 copy-done.3
  72.4 0.0 copy-done.4
  72.4 0.0 copy-done.5
  72.4 13.7 %update.1 = bf16[2,8,1024,128]{3,2,1,0:T(8,128)(2,1)} custom-call(s32[2]{0:T(128)S(1)} %copy-done.3, s32[2,64]{1,0:T(2,128)S(1)} %copy-done.4, s32[2,64]{1,0:T(2,128)S(1)} %copy-done.5, bf16[2,2,256,256]{3,2,1,0:T(8,128)(2,1)S(1)} %copy-done.1, bf16[2,2,4,4,128,256]{5,4,3,2,1,0:T(8,128)(2,1)S(1)} %get-tuple-element.17.x_ref, ...), custom_call_target="tpu_custom_call" | custom-call | tf_op jit(solution)/shard_map/update/pallas_call | solution.py:661
Async XLA Ops:
  0.0 2.2 %copy-start = (bf16[2,8,1,256,2,1,256]{6,4,5,3,2,1,0:T(2,128)(2,1)S(1)}, bf16[2,8,1,256,2,1,256]{6,4,5,3,2,1,0:T(2,128)(2,1)}, u32[]{:S(2)}) copy-start(bf16[2,8,1,256,2,1,256]{6,4,5,3,2,1,0:T(2,128)(2,1)} %param.5) | copy-start | bytes 12582916
  2.2 0.7 copy-start.2
  2.8 69.5 %copy-start.1 = (bf16[2,2,256,256]{3,2,1,0:T(8,128)(2,1)S(1)}, bf16[2,2,256,256]{3,2,1,0:T(8,128)(2,1)}, u32[]{:S(2)}) copy-start(bf16[2,2,256,256]{3,2,1,0:T(8,128)(2,1)} %inv_ref.1) | copy-start | bytes 1572868
  2.8 69.5 %copy-start.3 = (s32[2]{0:T(128)S(1)}, s32[2]{0:T(128)}, u32[]{:S(2)}) copy-start(s32[2]{0:T(128)} %piv_ref.5) | copy-start | bytes 28
  2.8 69.6 %copy-start.4 = (s32[2,64]{1,0:T(2,128)S(1)}, s32[2,64]{1,0:T(2,128)}, u32[]{:S(2)}) copy-start(s32[2,64]{1,0:T(2,128)} %cl_ref.1) | copy-start | bytes 1540
  2.9 69.6 %copy-start.5 = (s32[2,64]{1,0:T(2,128)S(1)}, s32[2,64]{1,0:T(2,128)}, u32[]{:S(2)}) copy-start(s32[2,64]{1,0:T(2,128)} %rl_ref.1) | copy-start | bytes 1540
